TPU v7x, 256 devices: a whole 4x4x8 slice. The times are simulated.
256 devices in a mesh: lon: 16 (over z_lo, y), lat: 16 (over x, z_hi, core).
Axes of the slice: x: 4, y: 4, z: 8 (z_hi: 2, z_lo: 4; z = z_hi * 4 + z_lo), core: 2. Of those that a mesh axis runs over, the one named last changes fastest.
Arguments:
- sample_deviations: float32 [32, 32, 128, 2048], P(None, None, 'lat', 'lon'), may hold values from -6 to 6
- east_courant: float32 [32, 128, 2048], P(None, 'lat', 'lon'), may hold values from -0.45 to 0.45
- north_courant: float32 [32, 128, 2048], P(None, 'lat', 'lon'), may hold values from -0.45 to 0.45
- production: float32 [32, 128, 2048], P(None, 'lat', 'lon'), may hold values from -1.8 to 1.8
- loss_rate: float32 [32, 128, 2048], P(None, 'lat', 'lon'), may hold values from 0.02 to 0.3
- entry_count: int32 [256], P(('lon', 'lat')), may hold values from 24 to 48, as said below
- entry_row: int32 [12288], P(('lon', 'lat')), may hold values from 0 to 7
- entry_block: int32 [12288], P(('lon', 'lat')), may hold values from 0 to 63
- path_weight: bfloat16 [12288, 128, 128], P(('lon', 'lat')), may hold values from 0 to 0.15234375
- observed: float32 [131072], P(('lon', 'lat')), may hold values from -288 to 288
- obs_var: float32 [131072], P(('lon', 'lat')), may hold values from 512 to 36864, as said below
Outputs:
- updated_samples: float32 [32, 32, 128, 2048], P(None, None, 'lat', 'lon')
- prior_samples_in_path_space: float32 [32, 131072], P(None, ('lon', 'lat'))
- scaled_innovation: float32 [131072], P(('lon', 'lat'))
Inputs may be any that keep to these rules, and one draw needn't show every extreme that they name: `entry_count`: live crossing slots of each tile; some tile has all 48 live in every draw. `obs_var`: positive.
All inputs are finite; a program needn't handle non-finite values.
Results may differ from a plain program's by a relative error of at most 0.0025.
Values sent between devices are 32-bit elements; how exact they have to be, the bound alone decides.
A program may use at most 64 MiB of HBM per device.

v0:
```python
import math

import jax
import jax.numpy as jnp
from jax import lax
from jax.sharding import PartitionSpec as P

ALTITUDE_LAYERS = 32
RAY_BLOCK = 128
BLOCKS_DEV = 4
SLOTS_TILE = 48


highest = lax.Precision.HIGHEST


def extended(x, sides, width, wrap):
    for axis, dim in sides:
        size, length = (lax.axis_size(axis), x.shape[dim])
        up = [(i, (i + 1) % size) for i in range(size if wrap else size - 1)]
        down = [(j, i) for i, j in up]
        last = lax.slice_in_dim(x, length - width, length, axis=dim)
        initial = lax.slice_in_dim(x, 0, width, axis=dim)
        before = lax.ppermute(last, axis, up)
        after = lax.ppermute(initial, axis, down)
        x = jnp.concatenate([before, x, after], axis=dim)
    return x


def advance(
    plasma_concentration,
    west_cell,
    east_cell,
    south_cell,
    north_cell,
    east_speed,
    north_speed,
    source,
    loss_rate,
):
    advected = (
        plasma_concentration
        - jnp.maximum(east_speed, 0.0) * (plasma_concentration - west_cell)
        - jnp.minimum(east_speed, 0.0) * (east_cell - plasma_concentration)
    )
    advected = (
        advected
        - jnp.maximum(north_speed, 0.0) * (plasma_concentration - south_cell)
        - jnp.minimum(north_speed, 0.0) * (north_cell - plasma_concentration)
    )
    return (1.0 - loss_rate) * advected + source


def analysis_weights(gram_sum, pull_sum):
    member_total = gram_sum.shape[0]
    identity = jnp.eye(member_total, dtype=gram_sum.dtype)
    factor_low = jnp.linalg.cholesky(gram_sum + (member_total - 1.0) * identity)
    halfway = lax.linalg.triangular_solve(factor_low, pull_sum[:, None], left_side=True, lower=True)
    mean_weights = lax.linalg.triangular_solve(
        factor_low, halfway, left_side=True, lower=True, transpose_a=True
    )
    inverse = lax.linalg.triangular_solve(factor_low, identity, left_side=True, lower=True)
    return mean_weights + math.sqrt(member_total - 1.0) * inverse.T


def ray_moments(ensemble, observed, obs_var):
    ray_mean = jnp.mean(ensemble, axis=0)
    spread = ensemble - ray_mean
    misfit = observed - ray_mean
    gram_sum = jnp.dot(spread / obs_var, spread.T, precision=highest)
    pull_sum = jnp.dot(spread, misfit / obs_var, precision=highest)
    return (gram_sum, pull_sum, misfit / jnp.sqrt(obs_var))


def per_device(
    sample_deviations,
    east_courant,
    north_courant,
    production,
    loss_rate,
    entry_count,
    entry_row,
    entry_block,
    path_weight,
    observed,
    obs_var,
):
    ensemble_size = sample_deviations.shape[0]
    plasma_concentration = sample_deviations
    for repeat in range(2):
        lon_framed = extended(plasma_concentration, (("lon", 3),), 1, True)
        lat_framed = extended(plasma_concentration, (("lat", 2),), 1, False)
        plasma_concentration = advance(
            plasma_concentration,
            lon_framed[..., :-2],
            lon_framed[..., 2:],
            lat_framed[..., :-2, :],
            lat_framed[..., 2:, :],
            east_courant,
            north_courant,
            production,
            loss_rate,
        )
    column_integral_total = (
        jnp.sum(plasma_concentration, axis=1) / math.sqrt(ALTITUDE_LAYERS)
    ).astype(jnp.bfloat16)
    picked = jnp.take(column_integral_total, entry_row, axis=1)
    partial_value = jnp.einsum(
        "mkc,kcr->kmr", picked, path_weight, preferred_element_type=jnp.float32
    )
    lat_size = lax.axis_size("lat")
    col_blocks = BLOCKS_DEV * lat_size
    live_slots = (jnp.arange(SLOTS_TILE) < entry_count[0]).astype(jnp.float32)
    slot_select = (entry_block[None, :] == jnp.arange(col_blocks)[:, None]).astype(
        jnp.float32
    ) * live_slots[None, :]
    summed = jnp.einsum("bk,kmr->mbr", slot_select, partial_value, precision=highest).reshape(
        ensemble_size, col_blocks * RAY_BLOCK
    )
    prior_samples_in_path_space = lax.psum_scatter(summed, "lat", scatter_dimension=1, tiled=True)
    gram_sum, pull_sum, scaled_innovation = ray_moments(
        prior_samples_in_path_space, observed, obs_var
    )
    gram_sum, pull_sum = lax.psum((gram_sum, pull_sum), ("lon", "lat"))
    transform = analysis_weights(gram_sum, pull_sum)
    raveled_grid_vector = plasma_concentration.reshape(ensemble_size, -1)
    centre = jnp.mean(raveled_grid_vector, axis=0)
    anomalies = raveled_grid_vector - centre
    updated_samples = centre + jnp.dot(transform.T, anomalies, precision=highest)
    return (
        updated_samples.reshape(plasma_concentration.shape),
        prior_samples_in_path_space,
        scaled_innovation,
    )


def solution(mesh):
    in_specs = (
        P(None, None, "lat", "lon"),
        P(None, "lat", "lon"),
        P(None, "lat", "lon"),
        P(None, "lat", "lon"),
        P(None, "lat", "lon"),
        P(("lon", "lat")),
        P(("lon", "lat")),
        P(("lon", "lat")),
        P(("lon", "lat"), None, None),
        P(("lon", "lat")),
        P(("lon", "lat")),
    )
    out_specs = (P(None, None, "lat", "lon"), P(None, ("lon", "lat")), P(("lon", "lat")))
    return jax.shard_map(
        per_device, mesh=mesh, in_specs=in_specs, out_specs=out_specs, check_vma=False
    )
```

profile of v0, /device:TPU:1, one launch (start us, length us, event | category | flops | bytes accessed | tf_op | source)
XLA Modules:
  0.0 319.0 jit_solution(5074626505289613322)
XLA Ops:
  7.2 0.0 copy-start
  7.2 0.0 reduce-scatter.2.cloned.1.call-start
  7.2 8.1 %fusion.64 = (f32[32,32,8,1]{3,2,1,0:T(8,128)}, f32[32,32,8,1]{3,2,1,0:T(8,128)}) fusion(f32[32,32,8,128]{3,2,1,0:T(8,128)} %param.11), kind=kLoop, calls=%fused_computation.101 | loop fusion | bytes 131072 | tf_op jit(solution)/shard_map/slice | solution.py:22
  15.3 3.2 %copy.180 = f32[32,32,8,1]{1,2,3,0:T(8,128)S(1)} copy(f32[32,32,8,1]{3,2,1,0:T(8,128)} %get-tuple-element.12) | data formatting | bytes 65536
  18.6 0.0 copy-start.8
  18.6 0.0 copy-start.4
  18.6 2.2 collective-permute-start
  20.8 3.8 %copy.181 = f32[32,32,8,1]{1,2,3,0:T(8,128)} copy(f32[32,32,8,1]{3,2,1,0:T(8,128)} %get-tuple-element.13) | data formatting | bytes 65536
  24.6 5.5 %collective-permute-start.1 = (f32[32,32,8,1]{1,2,3,0:T(8,128)}, f32[32,32,8,1]{1,2,3,0:T(8,128)}, u32[]{:S(2)}, u32[]{:S(2)}) collective-permute-start(f32[32,32,8,1]{1,2,3,0:T(8,128)} %copy.181), channel_id=1, source_target_pairs={{16,0},{32,16},{48,32},{64,48},{80,64},{96,80},{112,96},{128,112},... | collective-permute-start | bytes 98312 | tf_op jit(solution)/shard_map/ppermute | solution.py:25
  30.2 5.4 %fusion.65 = (f32[32,32,1,128]{3,2,1,0:T(1,128)}, f32[32,32,1,128]{3,2,1,0:T(1,128)}) fusion(f32[32,32,8,128]{3,2,1,0:T(8,128)} %param.11), kind=kLoop, calls=%fused_computation.102 | loop fusion | bytes 2097152 | tf_op jit(solution)/shard_map/slice | solution.py:22
  35.6 8.5 %collective-permute-start.2 = (f32[32,32,1,128]{3,1,2,0:T(8,128)}, f32[32,32,1,128]{3,1,2,0:T(8,128)S(1)}, u32[]{:S(2)}, u32[]{:S(2)}) collective-permute-start(f32[32,32,1,128]{3,1,2,0:T(8,128)} %bitcast.20), channel_id=1, source_target_pairs={{0,1},{1,2},{2,3},{3,4},{4,5},{5,6},{6,7},{7,8},{8,9},{9,10},{10,1... | collective-permute-start | bytes 1572872 | tf_op jit(solution)/shard_map/ppermute | solution.py:24
  44.1 1.9 collective-permute-start.3
  46.0 0.0 copy-done.3
  46.1 0.9 broadcast_maximum_fusion
  47.7 0.0 copy-start.2
  47.7 0.0 collective-permute-done
  47.7 3.8 %copy.159 = f32[32,32,8,1]{3,2,1,0:T(8,128)} copy(f32[32,32,8,1]{1,2,3,0:T(8,128)} %collective-permute-done) | data formatting | bytes 65536 | tf_op jit(solution)/shard_map/ppermute | solution.py:24
  51.5 0.0 collective-permute-done.1
  51.5 3.8 %copy.161 = f32[32,32,8,1]{3,2,1,0:T(8,128)} copy(f32[32,32,8,1]{1,2,3,0:T(8,128)} %collective-permute-done.1) | data formatting | bytes 65536 | tf_op jit(solution)/shard_map/ppermute | solution.py:25
  55.4 1.2 collective-permute-done.2
  56.6 6.3 %collective-permute-done.3 = f32[32,32,1,128]{3,1,2,0:T(8,128)S(1)} collective-permute-done((f32[32,32,1,128]{3,1,2,0:T(8,128)}, f32[32,32,1,128]{3,1,2,0:T(8,128)S(1)}, u32[]{:S(2)}, u32[]{:S(2)}) %collective-permute-start.3) | collective-permute-done | bytes 524320 | tf_op jit(solution)/shard_map/ppermute | solution.py:25
  62.9 12.7 %fusion.19 = f32[32,32,8,128]{3,2,1,0:T(8,128)S(1)} fusion(f32[32,32,8,128]{3,2,1,0:T(8,128)} %param.11, f32[32,32,1,128]{3,2,1,0:T(1,128)S(1)} %bitcast.69, f32[32,32,1,128]{3,2,1,0:T(1,128)S(1)} %bitcast.68, f32[32,32,8,1]{3,2,1,0:T(8,128)} %copy.161, f32[32,32,8,1]{3,2,1,0:T(8,128)} %copy.159, f32[32,8,128]{2,1,0:T(8,128)S(1)} %copy-done.2, ...), kind=kLoop, calls=%fused_computation.27 | loop fusion | flops 18874368 | bytes 10289152 | tf_op jit(solution)/shard_map/add | solution.py:51
  75.6 0.0 copy-start.1
  75.6 2.4 fusion.63
  78.0 1.9 collective-permute-start.6
  79.9 2.4 collective-permute-start.7
  82.3 4.9 %fusion.62 = (f32[32,32,8,1]{3,2,1,0:T(8,128)}, f32[32,32,8,1]{3,2,1,0:T(8,128)}) fusion(f32[32,32,8,128]{3,2,1,0:T(8,128)S(1)} %fusion.19), kind=kLoop, calls=%fused_computation.99 | loop fusion | bytes 131072 | tf_op jit(solution)/shard_map/slice | solution.py:22
  87.2 0.0 copy-done.1
  87.2 3.2 %copy.166 = f32[32,32,8,1]{1,2,3,0:T(8,128)S(1)} copy(f32[32,32,8,1]{3,2,1,0:T(8,128)} %get-tuple-element.8) | data formatting | bytes 65536 | tf_op jit(solution)/shard_map/slice | solution.py:22
  90.4 0.3 collective-permute-start.4
  90.7 3.8 %copy.168 = f32[32,32,8,1]{1,2,3,0:T(8,128)} copy(f32[32,32,8,1]{3,2,1,0:T(8,128)} %get-tuple-element.9) | data formatting | bytes 65536 | tf_op jit(solution)/shard_map/slice | solution.py:23
  94.5 5.4 %collective-permute-start.5 = (f32[32,32,8,1]{1,2,3,0:T(8,128)}, f32[32,32,8,1]{1,2,3,0:T(8,128)}, u32[]{:S(2)}, u32[]{:S(2)}) collective-permute-start(f32[32,32,8,1]{1,2,3,0:T(8,128)} %copy.168), channel_id=1, source_target_pairs={{16,0},{32,16},{48,32},{64,48},{80,64},{96,80},{112,96},{128,112},... | collective-permute-start | bytes 98312 | tf_op jit(solution)/shard_map/ppermute | solution.py:25
  99.9 1.5 collective-permute-done.4
  101.4 3.8 %copy.167 = f32[32,32,8,1]{3,2,1,0:T(8,128)} copy(f32[32,32,8,1]{1,2,3,0:T(8,128)} %collective-permute-done.4) | data formatting | bytes 65536 | tf_op jit(solution)/shard_map/ppermute | solution.py:24
  105.2 0.0 collective-permute-done.5
  105.2 3.9 %copy.169 = f32[32,32,8,1]{3,2,1,0:T(8,128)} copy(f32[32,32,8,1]{1,2,3,0:T(8,128)} %collective-permute-done.5) | data formatting | bytes 65536 | tf_op jit(solution)/shard_map/ppermute | solution.py:25
  109.0 0.0 collective-permute-done.6
  109.0 0.0 collective-permute-done.7
  109.0 15.0 %fusion.60 = (f32[32,8,128]{2,1,0:T(8,128)S(1)}, f32[32,8,128]{2,1,0:T(8,128)S(1)}, f32[32,32,8,128]{3,2,1,0:T(8,128)}) fusion(f32[32,8,128]{2,1,0:T(8,128)S(1)} %copy-done.2, f32[32,32,8,128]{3,2,1,0:T(8,128)} %copy-done.1, f32[32,32,1,128]{3,2,1,0:T(1,128)S(1)} %bitcast.67, f32[32,8,128]{2,1,0:T(8,128)S(1)} %get-tuple-element.19, ...), kind=kLoop, calls=%fused_computation.98 | loop fusion | flops 20905984 | bytes 10551296 | tf_op jit(solution)/shard_map/reduce_sum | solution.py:127
  124.1 0.6 gather_fusion
  124.7 0.0 copy-start.5
  124.7 0.0 copy-start.6
  124.7 0.6 fusion.34
  125.3 0.0 copy-done.7
  125.3 1.6 fusion.32
  126.9 1.6 copy.199
  128.5 0.0 reduce-scatter.2.cloned.1.call-update
  128.5 85.1 %reduce-scatter.2.cloned.1.call-done = f32[32,512]{1,0:T(8,128)} async-done(((f32[32,8192]{1,0:T(8,128)}), f32[32,512]{1,0:T(8,128)}) %reduce-scatter.2.cloned.1.call-update) | async-done | bytes 65552 | tf_op jit(solution)/shard_map/reduce_scatter | solution.py:120
  213.7 0.9 reduce_sum.29
  214.5 0.0 copy-done.6
  214.5 0.6 rsqrt_multiply_fusion
  215.1 1.1 fusion.40
  216.2 1.0 convolution_bitcast_fusion
  217.2 76.6 %all-reduce = (f32[32,32]{1,0:T(8,128)S(1)}, f32[32]{0:T(128)S(1)}) all-reduce(f32[32,32]{1,0:T(8,128)S(1)} %fusion.40, f32[32]{0:T(128)S(1)} %convolution_bitcast_fusion), channel_id=1, replica_groups=mesh['lon'=16,'lat'=16] {'lon','lat'}, use_global_device_ids=true, to_apply=%region_4.5 | all-reduce | flops 1056 | bytes 8448 | tf_op jit(solution)/shard_map/psum | solution.py:124
  293.8 0.1 copy.178
  293.9 2.9 cholesky.17
  296.9 0.6 compare_reduce_fusion
  297.5 0.7 fusion.49
  298.2 2.4 custom-call.10
  300.6 0.2 convolution_bitcast_fusion.2
  300.7 0.1 convolution_bitcast_fusion.1
  300.9 0.2 fusion.31
  301.1 8.3 %fusion.29 = f32[4,8,256,128]{3,1,2,0:T(8,128)S(1)} fusion(f32[32,32]{1,0:T(8,128)S(1)} %fusion.31, f32[4,8,256,128]{3,2,1,0:T(8,128)} %bitcast.62, f32[32768]{0:T(1024)S(1)} %multiply_bitcast_fusion), kind=kOutput, calls=%fused_computation.40 | convolution fusion | flops 404750336 | bytes 8523776 | tf_op jit(solution)/shard_map/dot_general | solution.py:129
  309.4 2.8 copy.186
  (17 shorter events, 0.1 us)
Async XLA Ops:
  7.2 117.5 %copy-start = (bf16[48,128,128]{2,1,0:T(8,128)(2,1)S(1)}, bf16[48,128,128]{2,1,0:T(8,128)(2,1)}, u32[]{:S(2)}) copy-start(bf16[48,128,128]{2,1,0:T(8,128)(2,1)} %param.19) | copy-start | bytes 4718596
  7.2 206.5 %reduce-scatter.2.cloned.1.call-start = ((), (), s32[]{:S(2)}) async-start(), calls=%async_computation.1 | async-start | bytes 1114112 | tf_op jit(solution)/shard_map/reduce_scatter | solution.py:120
  18.6 27.4 %copy-start.3 = (f32[32,8,128]{2,1,0:T(8,128)S(1)}, f32[32,8,128]{2,1,0:T(8,128)}, u32[]{:S(2)}) copy-start(f32[32,8,128]{2,1,0:T(8,128)} %param.15) | copy-start | bytes 393220
  18.6 27.5 %copy-start.8 = (s32[48]{0:T(128)S(1)}, s32[48]{0:T(128)}, u32[]{:S(2)}) copy-start(s32[48]{0:T(128)} %param.17) | copy-start | bytes 580
  18.6 27.5 %copy-start.4 = (f32[32,8,128]{2,1,0:T(8,128)S(1)}, f32[32,8,128]{2,1,0:T(8,128)}, u32[]{:S(2)}) copy-start(f32[32,8,128]{2,1,0:T(8,128)} %param.13) | copy-start | bytes 393220
  18.6 29.1 %collective-permute-start = (f32[32,32,8,1]{1,2,3,0:T(8,128)S(1)}, f32[32,32,8,1]{1,2,3,0:T(8,128)}, u32[]{:S(2)}, u32[]{:S(2)}) collective-permute-start(f32[32,32,8,1]{1,2,3,0:T(8,128)S(1)} %copy.180), channel_id=1, source_target_pairs={{0,16},{16,32},{32,48},{48,64},{64,80},{80,96},{96,112},{112,128},... | collective-permute-start | bytes 98312 | tf_op jit(solution)/shard_map/ppermute | solution.py:24
  24.6 26.9 %collective-permute-start.1 = (f32[32,32,8,1]{1,2,3,0:T(8,128)}, f32[32,32,8,1]{1,2,3,0:T(8,128)}, u32[]{:S(2)}, u32[]{:S(2)}) collective-permute-start(f32[32,32,8,1]{1,2,3,0:T(8,128)} %copy.181), channel_id=1, source_target_pairs={{16,0},{32,16},{48,32},{64,48},{80,64},{96,80},{112,96},{128,112},... | collective-permute-start | bytes 98312 | tf_op jit(solution)/shard_map/ppermute | solution.py:25
  35.6 21.0 %collective-permute-start.2 = (f32[32,32,1,128]{3,1,2,0:T(8,128)}, f32[32,32,1,128]{3,1,2,0:T(8,128)S(1)}, u32[]{:S(2)}, u32[]{:S(2)}) collective-permute-start(f32[32,32,1,128]{3,1,2,0:T(8,128)} %bitcast.20), channel_id=1, source_target_pairs={{0,1},{1,2},{2,3},{3,4},{4,5},{5,6},{6,7},{7,8},{8,9},{9,10},{10,1... | collective-permute-start | bytes 1572872 | tf_op jit(solution)/shard_map/ppermute | solution.py:24
  44.1 18.8 %collective-permute-start.3 = (f32[32,32,1,128]{3,1,2,0:T(8,128)}, f32[32,32,1,128]{3,1,2,0:T(8,128)S(1)}, u32[]{:S(2)}, u32[]{:S(2)}) collective-permute-start(f32[32,32,1,128]{3,1,2,0:T(8,128)} %bitcast.21), channel_id=1, source_target_pairs={{1,0},{2,1},{3,2},{4,3},{5,4},{6,5},{7,6},{8,7},{9,8},{10,9},{11,1... | collective-permute-start | bytes 1572872 | tf_op jit(solution)/shard_map/ppermute | solution.py:25
  47.7 15.2 %copy-start.2 = (f32[32,8,128]{2,1,0:T(8,128)S(1)}, f32[32,8,128]{2,1,0:T(8,128)}, u32[]{:S(2)}) copy-start(f32[32,8,128]{2,1,0:T(8,128)} %param.14) | copy-start | bytes 393220
  75.6 11.6 %copy-start.1 = (f32[32,32,8,128]{3,2,1,0:T(8,128)}, f32[32,32,8,128]{3,2,1,0:T(8,128)S(1)}, u32[]{:S(2)}) copy-start(f32[32,32,8,128]{3,2,1,0:T(8,128)S(1)} %fusion.19) | copy-start | bytes 12582916
  78.0 31.1 %collective-permute-start.6 = (f32[32,32,1,128]{3,1,2,0:T(8,128)}, f32[32,32,1,128]{3,1,2,0:T(8,128)S(1)}, u32[]{:S(2)}, u32[]{:S(2)}) collective-permute-start(f32[32,32,1,128]{3,1,2,0:T(8,128)} %bitcast.2), channel_id=1, source_target_pairs={{0,1},{1,2},{2,3},{3,4},{4,5},{5,6},{6,7},{7,8},{8,9},{9,10},{10,1... | collective-permute-start | bytes 1572872 | tf_op jit(solution)/shard_map/ppermute | solution.py:24
  79.9 29.1 %collective-permute-start.7 = (f32[32,32,1,128]{3,1,2,0:T(8,128)}, f32[32,32,1,128]{3,1,2,0:T(8,128)S(1)}, u32[]{:S(2)}, u32[]{:S(2)}) collective-permute-start(f32[32,32,1,128]{3,1,2,0:T(8,128)} %bitcast.4), channel_id=1, source_target_pairs={{1,0},{2,1},{3,2},{4,3},{5,4},{6,5},{7,6},{8,7},{9,8},{10,9},{11,1... | collective-permute-start | bytes 1572872 | tf_op jit(solution)/shard_map/ppermute | solution.py:25
  90.4 10.9 %collective-permute-start.4 = (f32[32,32,8,1]{1,2,3,0:T(8,128)S(1)}, f32[32,32,8,1]{1,2,3,0:T(8,128)}, u32[]{:S(2)}, u32[]{:S(2)}) collective-permute-start(f32[32,32,8,1]{1,2,3,0:T(8,128)S(1)} %copy.166), channel_id=1, source_target_pairs={{0,16},{16,32},{32,48},{48,64},{64,80},{80,96},{96,112},{112,128},... | collective-permute-start | bytes 98312 | tf_op jit(solution)/shard_map/ppermute | solution.py:24
  94.5 10.6 %collective-permute-start.5 = (f32[32,32,8,1]{1,2,3,0:T(8,128)}, f32[32,32,8,1]{1,2,3,0:T(8,128)}, u32[]{:S(2)}, u32[]{:S(2)}) collective-permute-start(f32[32,32,8,1]{1,2,3,0:T(8,128)} %copy.168), channel_id=1, source_target_pairs={{16,0},{32,16},{48,32},{64,48},{80,64},{96,80},{112,96},{128,112},... | collective-permute-start | bytes 98312 | tf_op jit(solution)/shard_map/ppermute | solution.py:25
  109.0 16.3 %copy-start.7 = (s32[48]{0:T(128)S(1)}, s32[48]{0:T(128)}, u32[]{:S(2)}) copy-start(s32[48]{0:T(128)} %param.18) | copy-start | bytes 580
  124.7 89.8 %copy-start.5 = (f32[512]{0:T(512)S(1)}, f32[512]{0:T(512)}, u32[]{:S(2)}) copy-start(f32[512]{0:T(512)} %param.20) | copy-start | bytes 6148
  124.7 89.8 %copy-start.6 = (f32[512]{0:T(512)S(1)}, f32[512]{0:T(512)}, u32[]{:S(2)}) copy-start(f32[512]{0:T(512)} %param.21) | copy-start | bytes 6148
Sparse Core Ops, SparseCore 0:
  128.6 85.0 reduce-scatter.1
where the time goes:
time: 320 us; the launch traced here: 319 us
  waiting for transfers between devices  94.2 us (29%)
  blocking collectives  76.6 us (24%)
  local copies, waits for them, and re-layouts  55.3 us (17%)
  other arithmetic  36.8 us (11%)
  starting transfers between devices  28.1 us (9%)
  between operations  15 us (5%)
  matrix products  13.1 us (4%)
    reduce_scatter x1, waiting for transfers between devices, per_device(): lax.psum_scatter(summed, 'lat', scatter_dimension=1, tiled=True)  85.1 us
    psum x1, blocking collectives, per_device(): gram_sum, pull_sum = lax.psum((gram_sum, pull_sum), ('lon', 'lat'))  76.6 us
    slice x5, local copies, waits for them, and re-layouts, extended(): last = lax.slice_in_dim(x, length - width, length, axis=dim)  24 us
    ppermute x4, starting transfers between devices, extended(): after = lax.ppermute(initial, axis, down)  15.2 us
    reduce_sum x1, other arithmetic, per_device(): centre = jnp.mean(raveled_grid_vector, axis=0)  15 us
    ppermute x4, starting transfers between devices, extended(): before = lax.ppermute(last, axis, up)  12.8 us
    add x1, other arithmetic, advance(): return (1.0 - loss_rate) * advected + source  12.7 us
    unnamed x22, local copies, waits for them, and re-layouts  11.5 us
  transfers between devices with their start and end apart: 9, of which 4 were waited for; matrix products, arithmetic and copies ran while one was open for 12% of the time, Pallas kernels for 0%

commit v1 on v0

v1 whole, which is shorter than its diff:
```python
import math

import jax
import jax.numpy as jnp
from jax import lax
from jax.experimental import pallas as pl
from jax.experimental.pallas import tpu as pltpu
from jax.sharding import PartitionSpec as P

MEMBERS = 32
LEVELS = 32
TILE_LAT = 8
LANES = 128
SLOTS_TILE = 48
COL_BLOCKS = 64
MESH = pl.DeviceIdType.MESH
VMEM = pltpu.VMEM
F32 = jnp.float32
BF16 = jnp.bfloat16


def extended(x, sides, width, wrap):
    for axis, dim in sides:
        size, length = (lax.axis_size(axis), x.shape[dim])
        up = [(i, (i + 1) % size) for i in range(size if wrap else size - 1)]
        down = [(j, i) for i, j in up]
        last = lax.slice_in_dim(x, length - width, length, axis=dim)
        initial = lax.slice_in_dim(x, 0, width, axis=dim)
        before = lax.ppermute(last, axis, up)
        after = lax.ppermute(initial, axis, down)
        x = jnp.concatenate([before, x, after], axis=dim)
    return x


def advance(n, west, east, south, north, east_speed, north_speed, source, loss_rate):
    advected = n - jnp.maximum(east_speed, 0.0) * (n - west) - jnp.minimum(east_speed, 0.0) * (east - n)
    advected = advected - jnp.maximum(north_speed, 0.0) * (n - south) - jnp.minimum(north_speed, 0.0) * (north - n)
    return (1.0 - loss_rate) * advected + source


def ray_kernel(count_ref, row_ref, block_ref, content_ref, weight_ref, summed_ref, part_ref):
    summed_ref[...] = jnp.zeros_like(summed_ref)
    for k in range(SLOTS_TILE):
        picked = content_ref[row_ref[k]]
        part_ref[k] = jnp.dot(picked, weight_ref[k], preferred_element_type=F32)
    for k in range(SLOTS_TILE):
        block = block_ref[k]
        live = k < count_ref[0]
        summed_ref[block] += jnp.where(live, part_ref[k], 0.0)


def ray_sums(entry_count, entry_row, entry_block, content, path_weight):
    smem = pl.BlockSpec(memory_space=pltpu.SMEM)
    vmem = pl.BlockSpec(memory_space=VMEM)
    return pl.pallas_call(
        ray_kernel,
        out_shape=jax.ShapeDtypeStruct((COL_BLOCKS, MEMBERS, LANES), F32),
        in_specs=[smem, smem, smem, vmem, vmem],
        out_specs=vmem,
        scratch_shapes=[VMEM((SLOTS_TILE, MEMBERS, LANES), F32)],
        compiler_params=pltpu.CompilerParams(vmem_limit_bytes=16 * 2**20),
        name="ray_sums",
    )(entry_count, entry_row, entry_block, content, path_weight)


def weights_from(total):
    rows = lax.broadcasted_iota(jnp.int32, (MEMBERS, LANES), 0)
    lanes = lax.broadcasted_iota(jnp.int32, (MEMBERS, LANES), 1)
    inverse_lanes = (lanes >= 64) & (lanes < 64 + MEMBERS)
    work = total + jnp.where(lanes == rows, MEMBERS - 1.0, 0.0) + jnp.where(lanes == rows + 64, 1.0, 0.0)
    for j in range(MEMBERS):
        column = jnp.broadcast_to(work[:, j : j + 1], (MEMBERS, LANES))
        pivot = column[j : j + 1, :]
        scale = jnp.where(rows > j, column, 0.0) * (1.0 / pivot)
        work = work - scale * work[j : j + 1, :]
    diagonal = jnp.sum(jnp.where(lanes == rows, work, 0.0), axis=1, keepdims=True)
    work = work / jnp.sqrt(diagonal)
    inverse = jnp.where(inverse_lanes, work, 0.0)
    halfway = work[:, MEMBERS : MEMBERS + 1]
    mean_weights = jnp.sum(inverse * halfway, axis=0, keepdims=True)
    transform = jnp.where(inverse_lanes, mean_weights + math.sqrt(MEMBERS - 1.0) * inverse, 0.0)
    rest = (1.0 - jnp.sum(transform, axis=1, keepdims=True)) * (1.0 / MEMBERS)
    return jnp.where(inverse_lanes, transform + rest, 0.0)


def analysis_kernel(
    summed_ref, observed_ref, var_ref, prior_ref, innovation_ref, weights_ref,
    own, from_core, from_x, half, from_z, g0, g1, g2, g3, r_core, r_x, r_y, r_z,
    own_sem, core_send, core_recv, x_send, x_recv, z_send, z_recv, a_send, a_recv,
):
    lon, lat = lax.axis_index("lon"), lax.axis_index("lat")
    x, z_hi, core = lat // 4, lax.rem(lat // 2, 2), lax.rem(lat, 2)
    z_lo, y = lon // 4, lax.rem(lon, 4)

    def x_peer(k):
        return (lon, lax.rem(lat + 4 * k, 16))

    def y_peer(k):
        return (z_lo * 4 + lax.rem(y + k, 4), lat)

    def z_peer(k):
        z = lax.rem(z_hi * 4 + z_lo + k, 8)
        return (lax.rem(z, 4) * 4 + y, x * 4 + (z // 4) * 2 + core)

    core_peer = (lon, lat + 1 - 2 * core)
    peers = [core_peer] + [x_peer(k) for k in (1, 2, 3)] + [y_peer(k) for k in (1, 2, 3)]
    peers += [z_peer(k) for k in range(1, 8)]
    barrier = pltpu.get_barrier_semaphore()
    for peer in peers:
        pl.semaphore_signal(barrier, inc=1, device_id=peer, device_id_type=MESH)
    order = (2, 1, 3, 0)
    local = []
    for j in order:
        copy = pltpu.make_async_copy(summed_ref.at[lax.rem(x + j, 4), :, core], own.at[j], own_sem.at[j])
        copy.start()
        local.append(copy)
    pl.semaphore_wait(barrier, len(peers))

    def send(src, dst, send_sem, recv_sem, peer):
        copy = pltpu.make_async_remote_copy(
            src_ref=src, dst_ref=dst, send_sem=send_sem, recv_sem=recv_sem, device_id=peer, device_id_type=MESH
        )
        copy.start()
        return copy

    core_copies = [
        send(summed_ref.at[lax.rem(x + j, 4), :, 1 - core], from_core.at[j], core_send.at[j], core_recv.at[j], core_peer)
        for j in order
    ]
    x_copies = []
    for i, j in enumerate(order):
        local[i].wait()
        core_copies[i].wait_recv()
        own[j] = own[j] + from_core[j]
        if j:
            x_copies.append(send(own.at[j], from_x.at[j - 1], x_send.at[j - 1], x_recv.at[j - 1], x_peer(j)))
    for copy in x_copies:
        copy.wait_recv()
    half[...] = own[0] + from_x[0] + from_x[1] + from_x[2]
    z_copy = send(half.at[1 - z_hi], from_z, z_send, z_recv, z_peer(4))
    z_copy.wait_recv()
    samples = half[z_hi] + from_z[...]

    spreads, scaled = [], []
    for b in range(4):
        block = samples[b * MEMBERS : (b + 1) * MEMBERS]
        prior_ref[:, b * LANES : (b + 1) * LANES] = block
        mean = jnp.sum(block, axis=0, keepdims=True) * (1.0 / MEMBERS)
        misfit = observed_ref[b : b + 1, :] - mean
        variance = var_ref[b : b + 1, :]
        innovation_ref[b : b + 1, :] = misfit / jnp.sqrt(variance)
        spread = block - mean
        spreads.append(jnp.concatenate([spread, jnp.broadcast_to(misfit, (MEMBERS, LANES)), jnp.zeros((64, LANES), F32)], axis=0))
        scaled.append(spread / variance)
    gram = lax.dot_general(
        jnp.concatenate(scaled, axis=1), jnp.concatenate(spreads, axis=1), (((1,), (1,)), ((), ())),
        precision=lax.Precision.HIGHEST, preferred_element_type=F32,
    )
    lanes = lax.broadcasted_iota(jnp.int32, (MEMBERS, LANES), 1)
    g0[...] = jnp.where(lanes <= MEMBERS, gram, 0.0)

    waits = []
    base = 0

    def exchange(source, landing, targets):
        nonlocal base
        copies = [
            send(source, landing.at[i], a_send.at[base + i], a_recv.at[base + i], target)
            for i, target in enumerate(targets)
        ]
        base += len(targets)
        for copy in copies:
            copy.wait_recv()
        waits.extend(copies)
        total = source[...]
        for i in range(len(targets)):
            total = total + landing[i]
        return total

    g1[...] = exchange(g0, r_core, [core_peer])
    g2[...] = exchange(g1, r_x, [x_peer(k) for k in (1, 2, 3)])
    g3[...] = exchange(g2, r_y, [y_peer(k) for k in (1, 2, 3)])
    total = exchange(g3, r_z, [z_peer(k) for k in range(1, 8)])
    weights_ref[...] = weights_from(total)
    for copy in core_copies + x_copies + [z_copy] + waits:
        copy.wait_send()


def analysis(summed, observed, obs_var):
    vmem = pl.BlockSpec(memory_space=VMEM)
    piece = (2, 4 * MEMBERS, LANES)
    dma = pltpu.SemaphoreType.DMA
    return pl.pallas_call(
        analysis_kernel,
        out_shape=(
            jax.ShapeDtypeStruct((MEMBERS, 4 * LANES), F32),
            jax.ShapeDtypeStruct((4, LANES), F32),
            jax.ShapeDtypeStruct((MEMBERS, LANES), F32),
        ),
        in_specs=[pl.BlockSpec(memory_space=pl.ANY), vmem, vmem],
        out_specs=(vmem, vmem, vmem),
        scratch_shapes=[
            VMEM((4,) + piece, F32), VMEM((4,) + piece, F32), VMEM((3,) + piece, F32), VMEM(piece, F32), VMEM(piece[1:], F32),
        ]
        + [VMEM((MEMBERS, LANES), F32)] * 4
        + [VMEM((n, MEMBERS, LANES), F32) for n in (1, 3, 3, 7)]
        + [dma((4,)), dma((4,)), dma((4,)), dma((3,)), dma((3,)), dma, dma, dma((14,)), dma((14,))],
        compiler_params=pltpu.CompilerParams(collective_id=1, has_side_effects=True, vmem_limit_bytes=16 * 2**20),
        name="analysis",
    )(summed.reshape(4, 2, 2, 4 * MEMBERS, LANES), observed.reshape(4, LANES), obs_var.reshape(4, LANES))


LEVEL_STEP = 4


def update_kernel(weights_ref, forecast_ref, out_ref, high_ref, low_ref):
    @pl.when(pl.program_id(0) == 0)
    def _():
        size = MEMBERS * TILE_LAT
        tall = jnp.concatenate(
            [jnp.broadcast_to(weights_ref[b : b + 1, :], (TILE_LAT, LANES)) for b in range(MEMBERS)], axis=0
        )
        rows = lax.broadcasted_iota(jnp.int32, (LANES, size), 0)
        lanes = lax.broadcasted_iota(jnp.int32, (LANES, size), 1)
        spread = (lanes // TILE_LAT + 64 == rows).astype(F32)
        wide = jnp.dot(tall, spread, precision=lax.Precision.HIGHEST, preferred_element_type=F32)
        r = lax.broadcasted_iota(jnp.int32, (size, size), 0)
        c = lax.broadcasted_iota(jnp.int32, (size, size), 1)
        wide = jnp.where(lax.rem(r, TILE_LAT) == lax.rem(c, TILE_LAT), wide, 0.0)
        high = wide.astype(BF16)
        high_ref[...] = high
        low_ref[...] = (wide - high.astype(F32)).astype(BF16)

    for level in range(LEVEL_STEP):
        values = forecast_ref[:, level].reshape(MEMBERS * TILE_LAT, LANES)
        high = values.astype(BF16)
        low = (values - high.astype(F32)).astype(BF16)
        out = jnp.dot(high_ref[...], high, preferred_element_type=F32)
        out += jnp.dot(high_ref[...], low, preferred_element_type=F32)
        out += jnp.dot(low_ref[...], high, preferred_element_type=F32)
        out_ref[:, level] = out.reshape(MEMBERS, TILE_LAT, LANES)


def update(weights, forecast):
    size = MEMBERS * TILE_LAT
    block = pl.BlockSpec((MEMBERS, LEVEL_STEP, TILE_LAT, LANES), lambda i: (0, i, 0, 0))
    return pl.pallas_call(
        update_kernel,
        grid=(LEVELS // LEVEL_STEP,),
        out_shape=jax.ShapeDtypeStruct(forecast.shape, F32),
        in_specs=[pl.BlockSpec((MEMBERS, LANES), lambda i: (0, 0)), block],
        out_specs=block,
        scratch_shapes=[VMEM((size, size), BF16), VMEM((size, size), BF16)],
        compiler_params=pltpu.CompilerParams(vmem_limit_bytes=16 * 2**20),
        name="update",
    )(weights, forecast)


def per_device(
    sample_deviations, east_courant, north_courant, production, loss_rate,
    entry_count, entry_row, entry_block, path_weight, observed, obs_var,
):
    n = sample_deviations
    for repeat in range(2):
        lon_framed = extended(n, (("lon", 3),), 1, True)
        lat_framed = extended(n, (("lat", 2),), 1, False)
        n = advance(
            n, lon_framed[..., :-2], lon_framed[..., 2:], lat_framed[..., :-2, :], lat_framed[..., 2:, :],
            east_courant, north_courant, production, loss_rate,
        )
    content = (jnp.sum(n, axis=1) / math.sqrt(LEVELS)).astype(BF16)
    content = jnp.transpose(content, (1, 0, 2))
    summed = ray_sums(entry_count, entry_row, entry_block, content, path_weight)
    prior, innovation, weights = analysis(summed, observed, obs_var)
    return update(weights, n), prior, innovation.reshape(4 * LANES)


def solution(mesh):
    in_specs = (
        P(None, None, "lat", "lon"),
        P(None, "lat", "lon"),
        P(None, "lat", "lon"),
        P(None, "lat", "lon"),
        P(None, "lat", "lon"),
        P(("lon", "lat")),
        P(("lon", "lat")),
        P(("lon", "lat")),
        P(("lon", "lat"), None, None),
        P(("lon", "lat")),
        P(("lon", "lat")),
    )
    out_specs = (P(None, None, "lat", "lon"), P(None, ("lon", "lat")), P(("lon", "lat")))
    return jax.shard_map(per_device, mesh=mesh, in_specs=in_specs, out_specs=out_specs, check_vma=False)
```

time: 320 us -> 160 us (0.50)
  waiting for transfers between devices: 94.2 us -> 0.16 us
  blocking collectives: 76.6 us -> 0 us
  Pallas kernels: 0 us -> 51.6 us
  between operations: 15 us -> 1.49 us
  matrix products: 13.1 us -> 0 us
  local copies, waits for them, and re-layouts: 55.3 us -> 44.7 us
  other arithmetic: 36.8 us -> 26.8 us
  starting transfers between devices: 28.1 us -> 33.5 us
    reduce_scatter x1 -> x0, waiting for transfers between devices: 85.1 us -> none  [per_device(): lax.psum_scatter(summed, 'lat', scatter_dimension=1, tiled=True)]
    psum x1 -> x0, blocking collectives: 76.6 us -> none  [per_device(): gram_sum, pull_sum = lax.psum((gram_sum, pull_sum), ('lon', 'lat'))]
    pallas_call x0 -> x3, Pallas kernels: none -> 51.6 us  [the longest x1 43.9 us: analysis(): pl.pallas_call(analysis_kernel, out_shape=(jax.ShapeDtypeStruct((MEMBERS,...]
    dot_general x5 -> x0, matrix products: 12.5 us -> none  [the longest x1 8.28 us: per_device(): jnp.dot(transform.T, anomalies, precision=highest)]
    ppermute x4, starting transfers between devices: 12.8 us -> 19.9 us  [extended(): before = lax.ppermute(last, axis, up)]
    another operation x5 -> x0, other arithmetic: 6.68 us -> none  [the longest x3 3.59 us: analysis_weights(): factor_low = jnp.linalg.cholesky(gram_sum + (member_total - 1.0) * identity)]
    ppermute x4, waiting for transfers between devices: 6.33 us -> 0.01 us  [extended(): after = lax.ppermute(initial, axis, down)]
    unnamed x22 -> x24, local copies, waits for them, and re-layouts: 11.5 us -> 7.75 us
  transfers between devices with their start and end apart: 9 -> 8, of which waited for: 4 -> 1; matrix products, arithmetic and copies ran while one was open for 12% -> 24% of each run, Pallas kernels for 0% -> 0%
where the time goes in v1:
time: 160 us; the launch traced here: 158 us
  Pallas kernels  51.6 us (32%)
  local copies, waits for them, and re-layouts  44.7 us (28%)
  starting transfers between devices  33.5 us (21%)
  other arithmetic  26.8 us (17%)
    pallas_call x1, Pallas kernels, analysis(): pl.pallas_call(analysis_kernel, out_shape=(jax.ShapeDtypeStruct((MEMBERS,...  43.9 us
    slice x5, local copies, waits for them, and re-layouts, extended(): last = lax.slice_in_dim(x, length - width, length, axis=dim)  21.7 us
    ppermute x4, starting transfers between devices, extended(): before = lax.ppermute(last, axis, up)  19.9 us
    reduce_sum x1, other arithmetic, per_device(): content = (jnp.sum(n, axis=1) / math.sqrt(LEVELS)).astype(BF16)  14.1 us
    ppermute x4, starting transfers between devices, extended(): after = lax.ppermute(initial, axis, down)  13.6 us
    add x1, other arithmetic, advance(): return (1.0 - loss_rate) * advected + source  12.6 us
    unnamed x24, local copies, waits for them, and re-layouts  7.75 us
    pallas_call x1, Pallas kernels, update(): pl.pallas_call(update_kernel, grid=(LEVELS // LEVEL_STEP,), out_shape=jax...  6.6 us
  transfers between devices with their start and end apart: 8, of which 1 were waited for; matrix products, arithmetic and copies ran while one was open for 24% of the time, Pallas kernels for 0%

profile of v1, /device:TPU:1, one launch (start us, length us, event | category | flops | bytes accessed | tf_op | source)
XLA Modules:
  0.0 158.2 jit_solution(1637205739686960896)
XLA Ops:
  0.6 4.4 %fusion.35 = (f32[32,32,1,128]{3,2,1,0:T(1,128)S(1)}, f32[32,32,1,128]{3,2,1,0:T(1,128)S(1)}) fusion(f32[32,32,8,128]{3,2,1,0:T(8,128)} %param.11), kind=kLoop, calls=%fused_computation.48 | loop fusion | bytes 2097152 | tf_op jit(solution)/shard_map/slice | solution.py:27
  5.1 10.2 %collective-permute-start.2 = (f32[32,32,1,128]{3,2,1,0:T(1,128)S(1)}, f32[32,32,1,128]{3,2,1,0:T(1,128)S(1)}, u32[]{:S(2)}, u32[]{:S(2)}) collective-permute-start(f32[32,32,1,128]{3,2,1,0:T(1,128)S(1)} %get-tuple-element.17), channel_id=1, source_target_pairs={{0,1},{1,2},{2,3},{3,4},{4,5},{5,6},{6,7},{7,8},{8,9},{9,10},{10,1... | collective-permute-start | bytes 1572872 | tf_op jit(solution)/shard_map/ppermute | solution.py:29
  15.3 1.9 %collective-permute-start.3 = (f32[32,32,1,128]{3,2,1,0:T(1,128)S(1)}, f32[32,32,1,128]{3,2,1,0:T(1,128)S(1)}, u32[]{:S(2)}, u32[]{:S(2)}) collective-permute-start(f32[32,32,1,128]{3,2,1,0:T(1,128)S(1)} %get-tuple-element.18), channel_id=1, source_target_pairs={{1,0},{2,1},{3,2},{4,3},{5,4},{6,5},{7,6},{8,7},{9,8},{10,9},{11,1... | collective-permute-start | bytes 1572872 | tf_op jit(solution)/shard_map/ppermute | solution.py:30
  17.2 8.0 %fusion.34 = (f32[32,32,8,1]{3,2,1,0:T(8,128)}, f32[32,32,8,1]{3,2,1,0:T(8,128)}) fusion(f32[32,32,8,128]{3,2,1,0:T(8,128)} %param.11), kind=kLoop, calls=%fused_computation.47 | loop fusion | bytes 131072 | tf_op jit(solution)/shard_map/slice | solution.py:27
  25.2 0.0 copy-start.8
  25.2 0.0 copy-start.9
  25.2 0.0 copy-start.7
  25.2 3.3 %copy.23 = f32[32,32,8,1]{1,2,3,0:T(8,128)S(1)} copy(f32[32,32,8,1]{3,2,1,0:T(8,128)} %get-tuple-element.15) | data formatting | bytes 65536
  28.5 1.4 collective-permute-start
  29.9 3.2 %copy.24 = f32[32,32,8,1]{1,2,3,0:T(8,128)S(1)} copy(f32[32,32,8,1]{3,2,1,0:T(8,128)} %get-tuple-element.16) | data formatting | bytes 65536
  33.1 4.1 %collective-permute-start.1 = (f32[32,32,8,1]{1,2,3,0:T(8,128)S(1)}, f32[32,32,8,1]{1,2,3,0:T(8,128)S(1)}, u32[]{:S(2)}, u32[]{:S(2)}) collective-permute-start(f32[32,32,8,1]{1,2,3,0:T(8,128)S(1)} %copy.24), channel_id=1, source_target_pairs={{16,0},{32,16},{48,32},{64,48},{80,64},{96,80},{112,96},{128,112},... | collective-permute-start | bytes 98312 | tf_op jit(solution)/shard_map/ppermute | solution.py:30
  37.2 0.0 copy-done.8
  37.2 0.0 copy-done.9
  37.3 0.0 copy-done.7
  37.3 0.0 copy-start.6
  37.3 0.0 collective-permute-done
  37.3 3.0 %copy.15 = f32[32,32,8,1]{3,2,1,0:T(8,128)} copy(f32[32,32,8,1]{1,2,3,0:T(8,128)S(1)} %collective-permute-done) | data formatting | bytes 65536 | tf_op jit(solution)/shard_map/ppermute | solution.py:29
  40.3 0.0 collective-permute-done.1
  40.3 3.0 %copy.17 = f32[32,32,8,1]{3,2,1,0:T(8,128)} copy(f32[32,32,8,1]{1,2,3,0:T(8,128)S(1)} %collective-permute-done.1) | data formatting | bytes 65536 | tf_op jit(solution)/shard_map/ppermute | solution.py:30
  43.3 0.0 collective-permute-done.2
  43.3 0.0 collective-permute-done.3
  43.3 0.0 copy-done.6
  43.3 12.6 %fusion.18 = f32[32,32,8,128]{3,2,1,0:T(8,128)S(1)} fusion(f32[32,32,8,128]{3,2,1,0:T(8,128)} %param.11, f32[32,32,1,128]{3,2,1,0:T(1,128)S(1)} %collective-permute-done.3, f32[32,32,1,128]{3,2,1,0:T(1,128)S(1)} %collective-permute-done.2, f32[32,32,8,1]{3,2,1,0:T(8,128)} %copy.17, f32[32,32,8,1]{3,2,1,0:T(8,128)} %copy.15, f32[32,8,128]{2,1,0:T(8,128)S(1)} %copy-done.6, ...), kind=kLoop, calls=%fused_computation.23 | loop fusion | flops 18874368 | bytes 10289152 | tf_op jit(solution)/shard_map/add | solution.py:38
  56.0 0.0 copy-start.5
  56.0 1.1 fusion.33
  57.1 8.1 %collective-permute-start.6 = (f32[32,32,1,128]{3,2,1,0:T(1,128)S(1)}, f32[32,32,1,128]{3,2,1,0:T(1,128)S(1)}, u32[]{:S(2)}, u32[]{:S(2)}) collective-permute-start(f32[32,32,1,128]{3,2,1,0:T(1,128)S(1)} %get-tuple-element.13), channel_id=1, source_target_pairs={{0,1},{1,2},{2,3},{3,4},{4,5},{5,6},{6,7},{7,8},{8,9},{9,10},{10,1... | collective-permute-start | bytes 1572872 | tf_op jit(solution)/shard_map/ppermute | solution.py:29
  65.2 1.9 %collective-permute-start.7 = (f32[32,32,1,128]{3,2,1,0:T(1,128)S(1)}, f32[32,32,1,128]{3,2,1,0:T(1,128)S(1)}, u32[]{:S(2)}, u32[]{:S(2)}) collective-permute-start(f32[32,32,1,128]{3,2,1,0:T(1,128)S(1)} %get-tuple-element.14), channel_id=1, source_target_pairs={{1,0},{2,1},{3,2},{4,3},{5,4},{6,5},{7,6},{8,7},{9,8},{10,9},{11,1... | collective-permute-start | bytes 1572872 | tf_op jit(solution)/shard_map/ppermute | solution.py:30
  67.1 5.0 %fusion.32 = (f32[32,32,8,1]{3,2,1,0:T(8,128)}, f32[32,32,8,1]{3,2,1,0:T(8,128)}) fusion(f32[32,32,8,128]{3,2,1,0:T(8,128)S(1)} %fusion.18), kind=kLoop, calls=%fused_computation.45 | loop fusion | bytes 131072 | tf_op jit(solution)/shard_map/slice | solution.py:27
  72.1 0.0 copy-done.5
  72.1 3.2 %copy.18 = f32[32,32,8,1]{1,2,3,0:T(8,128)S(1)} copy(f32[32,32,8,1]{3,2,1,0:T(8,128)} %get-tuple-element.11) | data formatting | bytes 65536 | tf_op jit(solution)/shard_map/slice | solution.py:27
  75.3 0.3 collective-permute-start.4
  75.6 3.2 %copy.20 = f32[32,32,8,1]{1,2,3,0:T(8,128)S(1)} copy(f32[32,32,8,1]{3,2,1,0:T(8,128)} %get-tuple-element.12) | data formatting | bytes 65536 | tf_op jit(solution)/shard_map/slice | solution.py:28
  78.8 5.6 %collective-permute-start.5 = (f32[32,32,8,1]{1,2,3,0:T(8,128)S(1)}, f32[32,32,8,1]{1,2,3,0:T(8,128)S(1)}, u32[]{:S(2)}, u32[]{:S(2)}) collective-permute-start(f32[32,32,8,1]{1,2,3,0:T(8,128)S(1)} %copy.20), channel_id=1, source_target_pairs={{16,0},{32,16},{48,32},{64,48},{80,64},{96,80},{112,96},{128,112},... | collective-permute-start | bytes 98312 | tf_op jit(solution)/shard_map/ppermute | solution.py:30
  85.0 0.1 collective-permute-done.4
  85.2 3.0 %copy.19 = f32[32,32,8,1]{3,2,1,0:T(8,128)} copy(f32[32,32,8,1]{1,2,3,0:T(8,128)S(1)} %collective-permute-done.4) | data formatting | bytes 65536 | tf_op jit(solution)/shard_map/ppermute | solution.py:29
  88.2 0.0 collective-permute-done.5
  88.2 3.0 %copy.21 = f32[32,32,8,1]{3,2,1,0:T(8,128)} copy(f32[32,32,8,1]{1,2,3,0:T(8,128)S(1)} %collective-permute-done.5) | data formatting | bytes 65536 | tf_op jit(solution)/shard_map/ppermute | solution.py:30
  91.2 0.0 copy-start
  91.2 0.0 copy-start.3
  91.2 0.0 copy-start.4
  91.2 0.0 copy-start.1
  91.2 0.0 copy-start.2
  91.2 0.0 collective-permute-done.6
  91.2 0.0 collective-permute-done.7
  91.2 14.1 %fusion.30 = (f32[32,8,128]{2,1,0:T(8,128)S(1)}, f32[32,32,8,128]{3,2,1,0:T(8,128)S(1)}) fusion(f32[32,8,128]{2,1,0:T(8,128)S(1)} %copy-done.6, f32[32,32,8,128]{3,2,1,0:T(8,128)} %copy-done.5, f32[32,32,1,128]{3,2,1,0:T(1,128)S(1)} %collective-permute-done.7, f32[32,8,128]{2,1,0:T(8,128)S(1)} %get-tuple-element.22, ...), kind=kLoop, calls=%fused_computation.44 | loop fusion | flops 19890176 | bytes 10420224 | tf_op jit(solution)/shard_map/reduce_sum | solution.py:271
  105.4 0.0 copy-done
  105.4 0.0 copy-done.3
  105.4 0.0 copy-done.4
  105.4 1.1 ray_sums.1
  106.5 0.0 copy-done.1
  106.5 0.0 copy-done.2
  106.5 43.9 %analysis.1 = (f32[32,512]{1,0:T(8,128)S(1)}, f32[4,128]{1,0:T(4,128)S(1)}, f32[32,128]{1,0:T(8,128)S(1)}) custom-call(f32[4,2,2,128,128]{4,3,2,1,0:T(8,128)S(1)} %bitcast.6, f32[4,128]{1,0:T(4,128)S(1)} %bitcast.7, f32[4,128]{1,0:T(4,128)S(1)} %bitcast.8), custom_call_target="tpu_custom_call" | custom-call | tf_op jit(solution)/shard_map/analysis/pallas_call | solution.py:193
  150.4 6.6 %update.1 = f32[32,32,8,128]{3,2,1,0:T(8,128)} custom-call(f32[32,128]{1,0:T(8,128)S(1)} %get-tuple-element.6.weights_ref, f32[32,32,8,128]{3,2,1,0:T(8,128)S(1)} %get-tuple-element.10.forecast_ref), custom_call_target="tpu_custom_call" | custom-call | tf_op jit(solution)/shard_map/update/pallas_call | solution.py:247
  157.0 0.6 copy.33
  157.6 0.6 copy.34
  (3 shorter events, 0.1 us)
Async XLA Ops:
  5.1 38.3 %collective-permute-start.2 = (f32[32,32,1,128]{3,2,1,0:T(1,128)S(1)}, f32[32,32,1,128]{3,2,1,0:T(1,128)S(1)}, u32[]{:S(2)}, u32[]{:S(2)}) collective-permute-start(f32[32,32,1,128]{3,2,1,0:T(1,128)S(1)} %get-tuple-element.17), channel_id=1, source_target_pairs={{0,1},{1,2},{2,3},{3,4},{4,5},{5,6},{6,7},{7,8},{8,9},{9,10},{10,1... | collective-permute-start | bytes 1572872 | tf_op jit(solution)/shard_map/ppermute | solution.py:29
  15.3 28.1 %collective-permute-start.3 = (f32[32,32,1,128]{3,2,1,0:T(1,128)S(1)}, f32[32,32,1,128]{3,2,1,0:T(1,128)S(1)}, u32[]{:S(2)}, u32[]{:S(2)}) collective-permute-start(f32[32,32,1,128]{3,2,1,0:T(1,128)S(1)} %get-tuple-element.18), channel_id=1, source_target_pairs={{1,0},{2,1},{3,2},{4,3},{5,4},{6,5},{7,6},{8,7},{9,8},{10,9},{11,1... | collective-permute-start | bytes 1572872 | tf_op jit(solution)/shard_map/ppermute | solution.py:30
  25.2 12.0 %copy-start.8 = (f32[32,8,128]{2,1,0:T(8,128)S(1)}, f32[32,8,128]{2,1,0:T(8,128)}, u32[]{:S(2)}) copy-start(f32[32,8,128]{2,1,0:T(8,128)} %param.13) | copy-start | bytes 393220
  25.2 12.0 %copy-start.9 = (f32[32,8,128]{2,1,0:T(8,128)S(1)}, f32[32,8,128]{2,1,0:T(8,128)}, u32[]{:S(2)}) copy-start(f32[32,8,128]{2,1,0:T(8,128)} %param.12) | copy-start | bytes 393220
  25.2 12.1 %copy-start.7 = (f32[32,8,128]{2,1,0:T(8,128)S(1)}, f32[32,8,128]{2,1,0:T(8,128)}, u32[]{:S(2)}) copy-start(f32[32,8,128]{2,1,0:T(8,128)} %param.15) | copy-start | bytes 393220
  28.5 8.8 %collective-permute-start = (f32[32,32,8,1]{1,2,3,0:T(8,128)S(1)}, f32[32,32,8,1]{1,2,3,0:T(8,128)S(1)}, u32[]{:S(2)}, u32[]{:S(2)}) collective-permute-start(f32[32,32,8,1]{1,2,3,0:T(8,128)S(1)} %copy.23), channel_id=1, source_target_pairs={{0,16},{16,32},{32,48},{48,64},{64,80},{80,96},{96,112},{112,128},... | collective-permute-start | bytes 98312 | tf_op jit(solution)/shard_map/ppermute | solution.py:29
  33.1 7.2 %collective-permute-start.1 = (f32[32,32,8,1]{1,2,3,0:T(8,128)S(1)}, f32[32,32,8,1]{1,2,3,0:T(8,128)S(1)}, u32[]{:S(2)}, u32[]{:S(2)}) collective-permute-start(f32[32,32,8,1]{1,2,3,0:T(8,128)S(1)} %copy.24), channel_id=1, source_target_pairs={{16,0},{32,16},{48,32},{64,48},{80,64},{96,80},{112,96},{128,112},... | collective-permute-start | bytes 98312 | tf_op jit(solution)/shard_map/ppermute | solution.py:30
  37.3 6.0 %copy-start.6 = (f32[32,8,128]{2,1,0:T(8,128)S(1)}, f32[32,8,128]{2,1,0:T(8,128)}, u32[]{:S(2)}) copy-start(f32[32,8,128]{2,1,0:T(8,128)} %param.14) | copy-start | bytes 393220
  56.0 16.1 %copy-start.5 = (f32[32,32,8,128]{3,2,1,0:T(8,128)}, f32[32,32,8,128]{3,2,1,0:T(8,128)S(1)}, u32[]{:S(2)}) copy-start(f32[32,32,8,128]{3,2,1,0:T(8,128)S(1)} %fusion.18) | copy-start | bytes 12582916
  57.1 34.1 %collective-permute-start.6 = (f32[32,32,1,128]{3,2,1,0:T(1,128)S(1)}, f32[32,32,1,128]{3,2,1,0:T(1,128)S(1)}, u32[]{:S(2)}, u32[]{:S(2)}) collective-permute-start(f32[32,32,1,128]{3,2,1,0:T(1,128)S(1)} %get-tuple-element.13), channel_id=1, source_target_pairs={{0,1},{1,2},{2,3},{3,4},{4,5},{5,6},{6,7},{7,8},{8,9},{9,10},{10,1... | collective-permute-start | bytes 1572872 | tf_op jit(solution)/shard_map/ppermute | solution.py:29
  65.2 26.0 %collective-permute-start.7 = (f32[32,32,1,128]{3,2,1,0:T(1,128)S(1)}, f32[32,32,1,128]{3,2,1,0:T(1,128)S(1)}, u32[]{:S(2)}, u32[]{:S(2)}) collective-permute-start(f32[32,32,1,128]{3,2,1,0:T(1,128)S(1)} %get-tuple-element.14), channel_id=1, source_target_pairs={{1,0},{2,1},{3,2},{4,3},{5,4},{6,5},{7,6},{8,7},{9,8},{10,9},{11,1... | collective-permute-start | bytes 1572872 | tf_op jit(solution)/shard_map/ppermute | solution.py:30
  75.3 9.9 %collective-permute-start.4 = (f32[32,32,8,1]{1,2,3,0:T(8,128)S(1)}, f32[32,32,8,1]{1,2,3,0:T(8,128)S(1)}, u32[]{:S(2)}, u32[]{:S(2)}) collective-permute-start(f32[32,32,8,1]{1,2,3,0:T(8,128)S(1)} %copy.18), channel_id=1, source_target_pairs={{0,16},{16,32},{32,48},{48,64},{64,80},{80,96},{96,112},{112,128},... | collective-permute-start | bytes 98312 | tf_op jit(solution)/shard_map/ppermute | solution.py:29
  78.8 9.4 %collective-permute-start.5 = (f32[32,32,8,1]{1,2,3,0:T(8,128)S(1)}, f32[32,32,8,1]{1,2,3,0:T(8,128)S(1)}, u32[]{:S(2)}, u32[]{:S(2)}) collective-permute-start(f32[32,32,8,1]{1,2,3,0:T(8,128)S(1)} %copy.20), channel_id=1, source_target_pairs={{16,0},{32,16},{48,32},{64,48},{80,64},{96,80},{112,96},{128,112},... | collective-permute-start | bytes 98312 | tf_op jit(solution)/shard_map/ppermute | solution.py:30
  91.2 14.2 %copy-start = (bf16[48,128,128]{2,1,0:T(8,128)(2,1)S(1)}, bf16[48,128,128]{2,1,0:T(8,128)(2,1)}, u32[]{:S(2)}) copy-start(bf16[48,128,128]{2,1,0:T(8,128)(2,1)} %weight_ref.1) | copy-start | bytes 4718596
  91.2 14.2 %copy-start.3 = (s32[48]{0:T(128)S(1)}, s32[48]{0:T(128)}, u32[]{:S(2)}) copy-start(s32[48]{0:T(128)} %row_ref.1) | copy-start | bytes 580
  91.2 14.2 %copy-start.4 = (s32[48]{0:T(128)S(1)}, s32[48]{0:T(128)}, u32[]{:S(2)}) copy-start(s32[48]{0:T(128)} %block_ref.1) | copy-start | bytes 580
  91.2 15.3 %copy-start.1 = (f32[512]{0:T(512)S(1)}, f32[512]{0:T(512)}, u32[]{:S(2)}) copy-start(f32[512]{0:T(512)} %param.20) | copy-start | bytes 6148
  91.2 15.3 %copy-start.2 = (f32[512]{0:T(512)S(1)}, f32[512]{0:T(512)}, u32[]{:S(2)}) copy-start(f32[512]{0:T(512)} %param.21) | copy-start | bytes 6148

commit v2 on v1

--- a/solution.py
+++ b/solution.py
@@ -19,23 +19,265 @@
 BF16 = jnp.bfloat16
 
 
-def extended(x, sides, width, wrap):
-    for axis, dim in sides:
-        size, length = (lax.axis_size(axis), x.shape[dim])
-        up = [(i, (i + 1) % size) for i in range(size if wrap else size - 1)]
-        down = [(j, i) for i, j in up]
-        last = lax.slice_in_dim(x, length - width, length, axis=dim)
-        initial = lax.slice_in_dim(x, 0, width, axis=dim)
-        before = lax.ppermute(last, axis, up)
-        after = lax.ppermute(initial, axis, down)
-        x = jnp.concatenate([before, x, after], axis=dim)
-    return x
-
-
-def advance(n, west, east, south, north, east_speed, north_speed, source, loss_rate):
-    advected = n - jnp.maximum(east_speed, 0.0) * (n - west) - jnp.minimum(east_speed, 0.0) * (east - n)
-    advected = advected - jnp.maximum(north_speed, 0.0) * (n - south) - jnp.minimum(north_speed, 0.0) * (north - n)
-    return (1.0 - loss_rate) * advected + source
+CHUNKS = 8
+CHUNK = LEVELS // CHUNKS
+BATCH = 32
+PAIRS = MEMBERS // 2
+
+
+def forecast_kernel(
+    east_ref, north_ref, source_ref, loss_ref, n_ref, out_ref, content_ref,
+    coefs, own, beyond, result, edges, to_east, to_west, edges_west, edges_east, beyond_west, beyond_east,
+    coef_edges, coef_west, coef_east, coef_beyond, frame0, frame_beyond, frame1, total,
+    load_sem, coef_sem, store_sem, small_send, small_recv, up_send, up_recv, down_send, down_recv,
+):
+    lon, lat = lax.axis_index("lon"), lax.axis_index("lat")
+    east, west = lax.rem(lon + 1, 16), lax.rem(lon + 15, 16)
+    north, south = lax.rem(lat + 1, 16), lax.rem(lat + 15, 16)
+    has_north, has_south = lat < 15, lat > 0
+    coef_loads = [
+        pltpu.make_async_copy(ref, coefs.at[i], coef_sem.at[i])
+        for i, ref in enumerate((east_ref, north_ref, source_ref, loss_ref))
+    ]
+    for item in coef_loads:
+        item.start()
+    half = pl.ds(0, MEMBERS // 2), pl.ds(MEMBERS // 2, MEMBERS // 2)
+    loads = [pltpu.make_async_copy(n_ref.at[part], own.at[part], load_sem.at[i]) for i, part in enumerate(half)]
+    for item in loads:
+        item.start()
+    barrier = pltpu.get_barrier_semaphore()
+    for peer in [(east, lat), (west, lat)] + [(i, j) for j in (north, south) for i in (lon, east, west)]:
+        pl.semaphore_signal(barrier, inc=1, device_id=peer, device_id_type=MESH)
+
+
+    def clear(part):
+        size = part.size
+        coef_beyond[:, :, part] = jnp.zeros((4, LEVELS, size, LANES), F32)
+        beyond_west[:, part] = jnp.zeros((PAIRS, size, LANES), F32)
+        beyond_east[:, part] = jnp.zeros((PAIRS, size, LANES), F32)
+
+        @pl.loop(0, MEMBERS)
+        def _(m):
+            beyond[m, :, part] = jnp.zeros((LEVELS, size, LANES), F32)
+
+    clear(pl.ds(2, TILE_LAT - 4))
+
+    @pl.when(lat == 15)
+    def _():
+        clear(pl.ds(0, 2))
+
+    @pl.when(lat == 0)
+    def _():
+        clear(pl.ds(TILE_LAT - 2, 2))
+
+    lanes = lax.broadcasted_iota(jnp.int32, (TILE_LAT, LANES), 1)
+    rows = lax.broadcasted_iota(jnp.int32, (TILE_LAT, LANES), 0)
+    group, slot = lanes // 4, lax.rem(lanes, 4)
+    is_first, is_last = rows == 0, rows == TILE_LAT - 1
+
+    def packed(ref, part):
+        out = jnp.zeros((ref[part, 0].shape[0], TILE_LAT, LANES), F32)
+        for level in range(LEVELS):
+            out = jnp.where(group == level, pltpu.roll(ref[part, level], (4 * level + 2) % LANES, 2), out)
+        return out
+
+    for item in coef_loads:
+        item.wait()
+    coef_edges[...] = packed(coefs, pl.ds(0, 4))
+    for i, item in enumerate(loads):
+        item.wait()
+        edges[half[i]] = packed(own, half[i])
+    first, second = edges[half[0]], edges[half[1]]
+    to_east[...] = jnp.where(slot < 2, first, pltpu.roll(second, 2, 2))
+    to_west[...] = jnp.where(slot >= 2, first, pltpu.roll(second, LANES - 2, 2))
+    pl.semaphore_wait(barrier, 8)
+
+    def copy(src, dst, send_sem, recv_sem, peer):
+        return pltpu.make_async_remote_copy(
+            src_ref=src, dst_ref=dst, send_sem=send_sem, recv_sem=recv_sem, device_id=peer, device_id_type=MESH
+        )
+
+    def small(i, src, dst, peer):
+        return copy(src, dst, small_send.at[i], small_recv.at[i], peer)
+
+    last, initial = pl.ds(TILE_LAT - 1, 1), pl.ds(0, 1)
+    across = [
+        small(0, coef_edges, coef_west, (east, lat)),
+        small(1, coef_edges, coef_east, (west, lat)),
+        small(2, to_east, edges_west, (east, lat)),
+        small(3, to_west, edges_east, (west, lat)),
+    ]
+    up = [
+        small(4, to_east.at[:, last], beyond_west.at[:, last], (east, north)),
+        small(5, to_west.at[:, last], beyond_east.at[:, last], (west, north)),
+        small(6, coefs.at[:, :, last], coef_beyond.at[:, :, last], (lon, north)),
+    ]
+    down = [
+        small(7, to_east.at[:, initial], beyond_west.at[:, initial], (east, south)),
+        small(8, to_west.at[:, initial], beyond_east.at[:, initial], (west, south)),
+        small(9, coefs.at[:, :, initial], coef_beyond.at[:, :, initial], (lon, south)),
+    ]
+
+    def bulk_up(q):
+        levels = pl.ds(q * CHUNK, CHUNK)
+        part = pl.ds(TILE_LAT - 2, 2)
+        return copy(n_ref.at[:, levels, part], beyond.at[:, levels, part], up_send.at[q], up_recv.at[q], (lon, north))
+
+    def bulk_down(q):
+        levels = pl.ds(q * CHUNK, CHUNK)
+        part = pl.ds(0, 2)
+        return copy(n_ref.at[:, levels, part], beyond.at[:, levels, part], down_send.at[q], down_recv.at[q], (lon, south))
+
+    for item in across:
+        item.start()
+
+    @pl.when(has_north)
+    def _():
+        for item in up:
+            item.start()
+
+    @pl.when(has_south)
+    def _():
+        for item in down:
+            item.start()
+
+    for q in range(CHUNKS):
+
+        @pl.when(has_north)
+        def _():
+            bulk_up(q).start()
+
+        @pl.when(has_south)
+        def _():
+            bulk_down(q).start()
+
+    for item in across:
+        item.wait()
+
+    @pl.when(has_south)
+    def _():
+        for item in up:
+            item.wait_recv()
+
+    @pl.when(has_north)
+    def _():
+        for item in down:
+            item.wait_recv()
+
+    def prepared(u, v, source, loss):
+        keep = 1.0 - loss
+        return keep * (1.0 - jnp.abs(u) - jnp.abs(v)), keep * jnp.abs(u), keep * jnp.abs(v), source, u > 0.0, v > 0.0
+
+    def step(n, west_cell, east_cell, outside, prep):
+        centre, along, across_, source, from_west, from_south = prep
+        north_cell = pltpu.roll(jnp.where(is_first, outside, n), TILE_LAT - 1, 1)
+        south_cell = pltpu.roll(jnp.where(is_last, outside, n), 1, 1)
+        upwind_lon = jnp.where(from_west, west_cell, east_cell)
+        upwind_lat = jnp.where(from_south, south_cell, north_cell)
+        return centre * n + along * upwind_lon + across_ * upwind_lat + source
+
+    def framed_step(n, frame, outside, prep):
+        west_cell = pltpu.roll(jnp.where(lanes == LANES - 1, frame, n), 1, 2)
+        east_cell = pltpu.roll(jnp.where(lanes == 0, frame, n), LANES - 1, 2)
+        return step(n, west_cell, east_cell, outside, prep)
+
+    edge_prep = prepared(*[jnp.where(slot == 1, coef_west[i], coef_east[i]) for i in range(4)])
+
+    for i, part in enumerate(half):
+        mine, from_west, from_east = edges[part], edges_west[...], edges_east[...]
+        outside_west, outside_east = beyond_west[...], beyond_east[...]
+        if i:
+            from_west, outside_west = (pltpu.roll(v, LANES - 2, 2) for v in (from_west, outside_west))
+            from_east, outside_east = (pltpu.roll(v, 2, 2) for v in (from_east, outside_east))
+        frame = jnp.where(slot == 1, from_west, from_east)
+        outside = jnp.where(slot == 1, outside_west, outside_east)
+        west_cell = pltpu.roll(jnp.where(slot == 0, from_west, mine), 1, 2)
+        east_cell = pltpu.roll(jnp.where(slot == 3, from_east, mine), LANES - 1, 2)
+        frame0[part] = frame
+        frame_beyond[part] = outside
+        frame1[part] = step(frame, west_cell, east_cell, outside, edge_prep)
+    total[...] = jnp.zeros_like(total)
+
+    @pl.loop(0, CHUNKS)
+    def _(q):
+        @pl.when(has_south)
+        def _():
+            bulk_up(q).wait_recv()
+
+        @pl.when(has_north)
+        def _():
+            bulk_down(q).wait_recv()
+
+        @pl.loop(0, CHUNK)
+        def _(i):
+            level = q * CHUNK + i
+            prep = prepared(*[coefs[k, level] for k in range(4)])
+            prep_beyond = prepared(*[coef_beyond[k, level] for k in range(4)])
+            shift = lax.rem(2 * LANES - 2 - 4 * level, LANES)
+
+            @pl.loop(0, MEMBERS // BATCH)
+            def _(g):
+                part = pl.ds(g * BATCH, BATCH)
+                n, out = own[part, level], beyond[part, level]
+                n1 = framed_step(n, pltpu.roll(frame0[part], shift, 2), out, prep)
+                out1 = framed_step(out, pltpu.roll(frame_beyond[part], shift, 2), n, prep_beyond)
+                n2 = framed_step(n1, pltpu.roll(frame1[part], shift, 2), out1, prep)
+                result[part, level] = n2
+                total[part] += n2
+
+        levels = pl.ds(q * CHUNK, CHUNK)
+        pltpu.make_async_copy(result.at[:, levels], out_ref.at[:, levels], store_sem.at[q]).start()
+
+    flat = total.reshape(MEMBERS * TILE_LAT, LANES)
+    for y in range(TILE_LAT):
+        content_ref[y] = (flat[pl.ds(y, MEMBERS, stride=TILE_LAT), :] / math.sqrt(LEVELS)).astype(BF16)
+
+    @pl.when(has_north)
+    def _():
+        for item in up:
+            item.wait_send()
+        for q in range(CHUNKS):
+            bulk_up(q).wait_send()
+
+    @pl.when(has_south)
+    def _():
+        for item in down:
+            item.wait_send()
+        for q in range(CHUNKS):
+            bulk_down(q).wait_send()
+
+    for q in range(CHUNKS):
+        levels = pl.ds(q * CHUNK, CHUNK)
+        pltpu.make_async_copy(result.at[:, levels], out_ref.at[:, levels], store_sem.at[q]).wait()
+
+
+def forecast(n, east_courant, north_courant, production, loss_rate):
+    vmem = pl.BlockSpec(memory_space=VMEM)
+    hbm = pl.BlockSpec(memory_space=pl.ANY)
+    field = VMEM((MEMBERS, LEVELS, TILE_LAT, LANES), F32)
+    packs = VMEM((MEMBERS, TILE_LAT, LANES), F32)
+    pairs = VMEM((PAIRS, TILE_LAT, LANES), F32)
+    coef_packs = VMEM((4, TILE_LAT, LANES), F32)
+    dma = pltpu.SemaphoreType.DMA
+    return pl.pallas_call(
+        forecast_kernel,
+        out_shape=(
+            jax.ShapeDtypeStruct(n.shape, F32),
+            jax.ShapeDtypeStruct((TILE_LAT, MEMBERS, LANES), BF16),
+        ),
+        in_specs=[hbm] * 5,
+        out_specs=(hbm, vmem),
+        scratch_shapes=[VMEM((4, LEVELS, TILE_LAT, LANES), F32)]
+        + [field] * 3
+        + [packs] + [pairs] * 6
+        + [coef_packs] * 3
+        + [VMEM((4, LEVELS, TILE_LAT, LANES), F32)]
+        + [packs] * 4
+        + [dma((2,)), dma((4,)), dma((CHUNKS,)), dma((10,)), dma((10,))]
+        + [dma((CHUNKS,))] * 4,
+        compiler_params=pltpu.CompilerParams(collective_id=2, has_side_effects=True, vmem_limit_bytes=60 * 2**20),
+        name="forecast",
+    )(east_courant, north_courant, production, loss_rate, n)
 
 
 def ray_kernel(count_ref, row_ref, block_ref, content_ref, weight_ref, summed_ref, part_ref):
@@ -260,16 +502,7 @@
     sample_deviations, east_courant, north_courant, production, loss_rate,
     entry_count, entry_row, entry_block, path_weight, observed, obs_var,
 ):
-    n = sample_deviations
-    for repeat in range(2):
-        lon_framed = extended(n, (("lon", 3),), 1, True)
-        lat_framed = extended(n, (("lat", 2),), 1, False)
-        n = advance(
-            n, lon_framed[..., :-2], lon_framed[..., 2:], lat_framed[..., :-2, :], lat_framed[..., 2:, :],
-            east_courant, north_courant, production, loss_rate,
-        )
-    content = (jnp.sum(n, axis=1) / math.sqrt(LEVELS)).astype(BF16)
-    content = jnp.transpose(content, (1, 0, 2))
+    n, content = forecast(sample_deviations, east_courant, north_courant, production, loss_rate)
     summed = ray_sums(entry_count, entry_row, entry_block, content, path_weight)
     prior, innovation, weights = analysis(summed, observed, obs_var)
     return update(weights, n), prior, innovation.reshape(4 * LANES)

time: 160 us -> 119 us (0.74); the launches traced: 158 us -> 119 us
  Pallas kernels: 51.6 us -> 113 us
  local copies, waits for them, and re-layouts: 44.7 us -> 4.24 us
  starting transfers between devices: 33.5 us -> 0 us
  other arithmetic: 26.8 us -> 0 us
    pallas_call x0 -> x1, Pallas kernels: none -> 55.9 us  [forecast(): pl.pallas_call(forecast_kernel, out_shape=(jax.ShapeDtypeStruct(n.shape,...]
    ppermute x8 -> x0, starting transfers between devices: 33.5 us -> none  [the longest x4 19.9 us: extended(): before = lax.ppermute(last, axis, up)]
    slice x6 -> x0, local copies, waits for them, and re-layouts: 24.9 us -> none  [the longest x5 21.7 us: extended(): last = lax.slice_in_dim(x, length - width, length, axis=dim)]
    reduce_sum x1 -> x0, other arithmetic: 14.1 us -> none  [per_device(): content = (jnp.sum(n, axis=1) / math.sqrt(LEVELS)).astype(BF16)]
    add x1 -> x0, other arithmetic: 12.6 us -> none  [advance(): return (1.0 - loss_rate) * advected + source]
    ppermute x4 -> x0, local copies, waits for them, and re-layouts: 12 us -> none  [the longest x2 6.01 us: extended(): before = lax.ppermute(last, axis, up)]
    pallas_call x1, Pallas kernels: 43.9 us -> 49.9 us  [analysis(): pl.pallas_call(analysis_kernel, out_shape=(jax.ShapeDtypeStruct((MEMBERS,...]
    unnamed x24 -> x16, local copies, waits for them, and re-layouts: 7.75 us -> 4.24 us
  transfers between devices with their start and end apart: 8 -> 0, of which waited for: 1 -> 0; matrix products, arithmetic and copies ran while one was open for 24% -> 0% of each run, Pallas kernels for 0% -> 0%
where the time goes in v2:
time: 119 us
  Pallas kernels  113 us (95%)
  local copies, waits for them, and re-layouts  4.24 us (4%)
  between operations  1.51 us (1%)
    pallas_call x1, Pallas kernels, forecast(): pl.pallas_call(forecast_kernel, out_shape=(jax.ShapeDtypeStruct(n.shape,...  55.9 us
    pallas_call x1, Pallas kernels, analysis(): pl.pallas_call(analysis_kernel, out_shape=(jax.ShapeDtypeStruct((MEMBERS,...  49.9 us
    pallas_call x1, Pallas kernels, update(): pl.pallas_call(update_kernel, grid=(LEVELS // LEVEL_STEP,), out_shape=jax...  6.59 us
    unnamed x16, local copies, waits for them, and re-layouts  4.24 us

profile of v2, /device:TPU:1, one launch (start us, length us, event | category | flops | bytes accessed | tf_op | source)
XLA Modules:
  0.0 119.2 jit_solution(14694434378800329023)
XLA Ops:
  0.6 0.0 copy-start.4
  0.6 0.0 copy-start.3
  0.7 0.0 copy-start.1
  0.7 0.0 copy-start.6
  0.7 0.0 copy-start.5
  1.4 55.9 %forecast.1 = (f32[32,32,8,128]{3,2,1,0:T(8,128)}, bf16[8,32,128]{2,1,0:T(8,128)(2,1)}) custom-call(f32[32,8,128]{2,1,0:T(8,128)} %east_ref.1, f32[32,8,128]{2,1,0:T(8,128)} %north_ref.1, f32[32,8,128]{2,1,0:T(8,128)} %source_ref.1, f32[32,8,128]{2,1,0:T(8,128)} %loss_ref.1, f32[32,32,8,128]{3,2,1,0:T(8,128)} %n_ref.1), custom_call_target="tpu_custom_call" | custom-call | tf_op jit(solution)/shard_map/forecast/pallas_call | solution.py:262
  57.4 0.0 copy-done.1
  57.4 0.0 copy-done.6
  57.4 0.0 copy-done.5
  57.4 0.0 copy-start.2
  57.4 0.8 copy-done.2
  58.2 1.1 ray_sums.1
  59.3 0.0 copy-done.4
  59.3 0.0 copy-done.3
  59.3 49.9 %analysis.1 = (f32[32,512]{1,0:T(8,128)S(1)}, f32[4,128]{1,0:T(4,128)S(1)}, f32[32,128]{1,0:T(8,128)S(1)}) custom-call(f32[4,2,2,128,128]{4,3,2,1,0:T(8,128)S(1)} %bitcast.4, f32[4,128]{1,0:T(4,128)S(1)} %bitcast.5, f32[4,128]{1,0:T(4,128)S(1)} %bitcast.6), custom_call_target="tpu_custom_call" | custom-call | tf_op jit(solution)/shard_map/analysis/pallas_call | solution.py:435
  109.2 0.0 copy-start
  109.2 2.2 %copy-done = f32[32,32,8,128]{3,2,1,0:T(8,128)S(1)} copy-done((f32[32,32,8,128]{3,2,1,0:T(8,128)S(1)}, f32[32,32,8,128]{3,2,1,0:T(8,128)}, u32[]{:S(2)}) %copy-start) | copy-done | bytes 4194328
  111.4 6.6 %update.1 = f32[32,32,8,128]{3,2,1,0:T(8,128)} custom-call(f32[32,128]{1,0:T(8,128)S(1)} %get-tuple-element.9.weights_ref, f32[32,32,8,128]{3,2,1,0:T(8,128)S(1)} %copy-done), custom_call_target="tpu_custom_call" | custom-call | tf_op jit(solution)/shard_map/update/pallas_call | solution.py:489
  118.0 0.6 copy.17
  118.6 0.6 copy.18
Async XLA Ops:
  0.6 58.7 %copy-start.4 = (f32[512]{0:T(512)S(1)}, f32[512]{0:T(512)}, u32[]{:S(2)}) copy-start(f32[512]{0:T(512)} %param.21) | copy-start | bytes 6148
  0.6 58.7 %copy-start.3 = (f32[512]{0:T(512)S(1)}, f32[512]{0:T(512)}, u32[]{:S(2)}) copy-start(f32[512]{0:T(512)} %param.20) | copy-start | bytes 6148
  0.7 56.7 %copy-start.1 = (bf16[48,128,128]{2,1,0:T(8,128)(2,1)S(1)}, bf16[48,128,128]{2,1,0:T(8,128)(2,1)}, u32[]{:S(2)}) copy-start(bf16[48,128,128]{2,1,0:T(8,128)(2,1)} %weight_ref.1) | copy-start | bytes 4718596
  0.7 56.7 %copy-start.6 = (s32[48]{0:T(128)S(1)}, s32[48]{0:T(128)}, u32[]{:S(2)}) copy-start(s32[48]{0:T(128)} %block_ref.1) | copy-start | bytes 580
  0.7 56.7 %copy-start.5 = (s32[48]{0:T(128)S(1)}, s32[48]{0:T(128)}, u32[]{:S(2)}) copy-start(s32[48]{0:T(128)} %row_ref.1) | copy-start | bytes 580
  57.4 0.8 copy-start.2
  109.2 2.2 %copy-start = (f32[32,32,8,128]{3,2,1,0:T(8,128)S(1)}, f32[32,32,8,128]{3,2,1,0:T(8,128)}, u32[]{:S(2)}) copy-start(f32[32,32,8,128]{3,2,1,0:T(8,128)} %get-tuple-element.10.forecast_ref) | copy-start | bytes 12582916

commit v3 on v2

--- a/solution.py
+++ b/solution.py
@@ -26,21 +26,15 @@
 
 
 def forecast_kernel(
-    east_ref, north_ref, source_ref, loss_ref, n_ref, out_ref, content_ref,
-    coefs, own, beyond, result, edges, to_east, to_west, edges_west, edges_east, beyond_west, beyond_east,
+    coefs, n_ref, out_ref, content_ref,
+    own, beyond, edges, to_east, to_west, edges_west, edges_east, beyond_west, beyond_east,
     coef_edges, coef_west, coef_east, coef_beyond, frame0, frame_beyond, frame1, total,
-    load_sem, coef_sem, store_sem, small_send, small_recv, up_send, up_recv, down_send, down_recv,
+    load_sem, small_send, small_recv, up_send, up_recv, down_send, down_recv,
 ):
     lon, lat = lax.axis_index("lon"), lax.axis_index("lat")
     east, west = lax.rem(lon + 1, 16), lax.rem(lon + 15, 16)
     north, south = lax.rem(lat + 1, 16), lax.rem(lat + 15, 16)
     has_north, has_south = lat < 15, lat > 0
-    coef_loads = [
-        pltpu.make_async_copy(ref, coefs.at[i], coef_sem.at[i])
-        for i, ref in enumerate((east_ref, north_ref, source_ref, loss_ref))
-    ]
-    for item in coef_loads:
-        item.start()
     half = pl.ds(0, MEMBERS // 2), pl.ds(MEMBERS // 2, MEMBERS // 2)
     loads = [pltpu.make_async_copy(n_ref.at[part], own.at[part], load_sem.at[i]) for i, part in enumerate(half)]
     for item in loads:
@@ -81,8 +75,6 @@
             out = jnp.where(group == level, pltpu.roll(ref[part, level], (4 * level + 2) % LANES, 2), out)
         return out
 
-    for item in coef_loads:
-        item.wait()
     coef_edges[...] = packed(coefs, pl.ds(0, 4))
     for i, item in enumerate(loads):
         item.wait()
@@ -222,11 +214,8 @@
                 n1 = framed_step(n, pltpu.roll(frame0[part], shift, 2), out, prep)
                 out1 = framed_step(out, pltpu.roll(frame_beyond[part], shift, 2), n, prep_beyond)
                 n2 = framed_step(n1, pltpu.roll(frame1[part], shift, 2), out1, prep)
-                result[part, level] = n2
+                out_ref[part, level] = n2
                 total[part] += n2
-
-        levels = pl.ds(q * CHUNK, CHUNK)
-        pltpu.make_async_copy(result.at[:, levels], out_ref.at[:, levels], store_sem.at[q]).start()
 
     flat = total.reshape(MEMBERS * TILE_LAT, LANES)
     for y in range(TILE_LAT):
@@ -246,14 +235,10 @@
         for q in range(CHUNKS):
             bulk_down(q).wait_send()
 
-    for q in range(CHUNKS):
-        levels = pl.ds(q * CHUNK, CHUNK)
-        pltpu.make_async_copy(result.at[:, levels], out_ref.at[:, levels], store_sem.at[q]).wait()
-
 
 def forecast(n, east_courant, north_courant, production, loss_rate):
     vmem = pl.BlockSpec(memory_space=VMEM)
-    hbm = pl.BlockSpec(memory_space=pl.ANY)
+    hbm = pl.BlockSpec(memory_space=pltpu.HBM)
     field = VMEM((MEMBERS, LEVELS, TILE_LAT, LANES), F32)
     packs = VMEM((MEMBERS, TILE_LAT, LANES), F32)
     pairs = VMEM((PAIRS, TILE_LAT, LANES), F32)
@@ -265,19 +250,18 @@
             jax.ShapeDtypeStruct(n.shape, F32),
             jax.ShapeDtypeStruct((TILE_LAT, MEMBERS, LANES), BF16),
         ),
-        in_specs=[hbm] * 5,
-        out_specs=(hbm, vmem),
-        scratch_shapes=[VMEM((4, LEVELS, TILE_LAT, LANES), F32)]
-        + [field] * 3
+        in_specs=[vmem, hbm],
+        out_specs=(vmem, vmem),
+        scratch_shapes=[field] * 2
         + [packs] + [pairs] * 6
         + [coef_packs] * 3
         + [VMEM((4, LEVELS, TILE_LAT, LANES), F32)]
         + [packs] * 4
-        + [dma((2,)), dma((4,)), dma((CHUNKS,)), dma((10,)), dma((10,))]
+        + [dma((2,)), dma((10,)), dma((10,))]
         + [dma((CHUNKS,))] * 4,
-        compiler_params=pltpu.CompilerParams(collective_id=2, has_side_effects=True, vmem_limit_bytes=60 * 2**20),
+        compiler_params=pltpu.CompilerParams(collective_id=2, has_side_effects=True, vmem_limit_bytes=46 * 2**20),
         name="forecast",
-    )(east_courant, north_courant, production, loss_rate, n)
+    )(jnp.stack([east_courant, north_courant, production, loss_rate]), n)
 
 
 def ray_kernel(count_ref, row_ref, block_ref, content_ref, weight_ref, summed_ref, part_ref):
@@ -309,7 +293,13 @@
     rows = lax.broadcasted_iota(jnp.int32, (MEMBERS, LANES), 0)
     lanes = lax.broadcasted_iota(jnp.int32, (MEMBERS, LANES), 1)
     inverse_lanes = (lanes >= 64) & (lanes < 64 + MEMBERS)
-    work = total + jnp.where(lanes == rows, MEMBERS - 1.0, 0.0) + jnp.where(lanes == rows + 64, 1.0, 0.0)
+    square = jnp.concatenate(
+        [pltpu.roll(total[0:8], LANES - MEMBERS * k, 1) if k else total[0:8] for k in range(4)], axis=0
+    )
+    square = jnp.where(lanes < MEMBERS, square, 0.0)
+    pull = jnp.sum(jnp.where(lanes == rows, total[8:9], 0.0), axis=1, keepdims=True)
+    work = square + jnp.where(lanes == MEMBERS, pull, 0.0)
+    work = work + jnp.where(lanes == rows, MEMBERS - 1.0, 0.0) + jnp.where(lanes == rows + 64, 1.0, 0.0)
     for j in range(MEMBERS):
         column = jnp.broadcast_to(work[:, j : j + 1], (MEMBERS, LANES))
         pivot = column[j : j + 1, :]
@@ -327,7 +317,7 @@
 
 def analysis_kernel(
     summed_ref, observed_ref, var_ref, prior_ref, innovation_ref, weights_ref,
-    own, from_core, from_x, half, from_z, g0, g1, g2, g3, r_core, r_x, r_y, r_z,
+    own, from_core, from_x, half, from_z, g0, g1, g2, r_plane, r_y, r_z,
     own_sem, core_send, core_recv, x_send, x_recv, z_send, z_recv, a_send, a_recv,
 ):
     lon, lat = lax.axis_index("lon"), lax.axis_index("lat")
@@ -345,7 +335,10 @@
         return (lax.rem(z, 4) * 4 + y, x * 4 + (z // 4) * 2 + core)
 
     core_peer = (lon, lat + 1 - 2 * core)
-    peers = [core_peer] + [x_peer(k) for k in (1, 2, 3)] + [y_peer(k) for k in (1, 2, 3)]
+    across = lat + 1 - 2 * core
+    plane_peers = [core_peer] + [x_peer(k) for k in (1, 2, 3)]
+    plane_peers += [(lon, lax.rem(across + 4 * k, 16)) for k in (1, 2, 3)]
+    peers = plane_peers + [y_peer(k) for k in (1, 2, 3)]
     peers += [z_peer(k) for k in range(1, 8)]
     barrier = pltpu.get_barrier_semaphore()
     for peer in peers:
@@ -392,14 +385,18 @@
         variance = var_ref[b : b + 1, :]
         innovation_ref[b : b + 1, :] = misfit / jnp.sqrt(variance)
         spread = block - mean
-        spreads.append(jnp.concatenate([spread, jnp.broadcast_to(misfit, (MEMBERS, LANES)), jnp.zeros((64, LANES), F32)], axis=0))
-        scaled.append(spread / variance)
+        spreads.append(jnp.concatenate([spread, jnp.zeros((LANES - MEMBERS, LANES), F32)], axis=0))
+        scaled.append(jnp.concatenate([spread, jnp.broadcast_to(misfit, (8, LANES))], axis=0) / variance)
     gram = lax.dot_general(
         jnp.concatenate(scaled, axis=1), jnp.concatenate(spreads, axis=1), (((1,), (1,)), ((), ())),
         precision=lax.Precision.HIGHEST, preferred_element_type=F32,
     )
-    lanes = lax.broadcasted_iota(jnp.int32, (MEMBERS, LANES), 1)
-    g0[...] = jnp.where(lanes <= MEMBERS, gram, 0.0)
+    lanes = lax.broadcasted_iota(jnp.int32, gram.shape, 1)
+    square = jnp.where(lanes < MEMBERS, gram, 0.0)
+    g0[0:8] = sum(
+        pltpu.roll(square[8 * k : 8 * k + 8], MEMBERS * k, 1) if k else square[0:8] for k in range(4)
+    )
+    g0[8:9] = gram[MEMBERS : MEMBERS + 1]
 
     waits = []
     base = 0
@@ -419,10 +416,9 @@
             total = total + landing[i]
         return total
 
-    g1[...] = exchange(g0, r_core, [core_peer])
-    g2[...] = exchange(g1, r_x, [x_peer(k) for k in (1, 2, 3)])
-    g3[...] = exchange(g2, r_y, [y_peer(k) for k in (1, 2, 3)])
-    total = exchange(g3, r_z, [z_peer(k) for k in range(1, 8)])
+    g1[...] = exchange(g0, r_plane, plane_peers)
+    g2[...] = exchange(g1, r_y, [y_peer(k) for k in (1, 2, 3)])
+    total = exchange(g2, r_z, [z_peer(k) for k in range(1, 8)])
     weights_ref[...] = weights_from(total)
     for copy in core_copies + x_copies + [z_copy] + waits:
         copy.wait_send()
@@ -444,58 +440,77 @@
         scratch_shapes=[
             VMEM((4,) + piece, F32), VMEM((4,) + piece, F32), VMEM((3,) + piece, F32), VMEM(piece, F32), VMEM(piece[1:], F32),
         ]
-        + [VMEM((MEMBERS, LANES), F32)] * 4
-        + [VMEM((n, MEMBERS, LANES), F32) for n in (1, 3, 3, 7)]
-        + [dma((4,)), dma((4,)), dma((4,)), dma((3,)), dma((3,)), dma, dma, dma((14,)), dma((14,))],
+        + [VMEM((9, LANES), F32)] * 3
+        + [VMEM((n, 9, LANES), F32) for n in (7, 3, 7)]
+        + [dma((4,)), dma((4,)), dma((4,)), dma((3,)), dma((3,)), dma, dma, dma((17,)), dma((17,))],
         compiler_params=pltpu.CompilerParams(collective_id=1, has_side_effects=True, vmem_limit_bytes=16 * 2**20),
         name="analysis",
     )(summed.reshape(4, 2, 2, 4 * MEMBERS, LANES), observed.reshape(4, LANES), obs_var.reshape(4, LANES))
 
 
-LEVEL_STEP = 4
-
-
-def update_kernel(weights_ref, forecast_ref, out_ref, high_ref, low_ref):
-    @pl.when(pl.program_id(0) == 0)
-    def _():
-        size = MEMBERS * TILE_LAT
-        tall = jnp.concatenate(
-            [jnp.broadcast_to(weights_ref[b : b + 1, :], (TILE_LAT, LANES)) for b in range(MEMBERS)], axis=0
-        )
-        rows = lax.broadcasted_iota(jnp.int32, (LANES, size), 0)
-        lanes = lax.broadcasted_iota(jnp.int32, (LANES, size), 1)
-        spread = (lanes // TILE_LAT + 64 == rows).astype(F32)
-        wide = jnp.dot(tall, spread, precision=lax.Precision.HIGHEST, preferred_element_type=F32)
-        r = lax.broadcasted_iota(jnp.int32, (size, size), 0)
-        c = lax.broadcasted_iota(jnp.int32, (size, size), 1)
-        wide = jnp.where(lax.rem(r, TILE_LAT) == lax.rem(c, TILE_LAT), wide, 0.0)
-        high = wide.astype(BF16)
-        high_ref[...] = high
-        low_ref[...] = (wide - high.astype(F32)).astype(BF16)
-
-    for level in range(LEVEL_STEP):
-        values = forecast_ref[:, level].reshape(MEMBERS * TILE_LAT, LANES)
-        high = values.astype(BF16)
-        low = (values - high.astype(F32)).astype(BF16)
-        out = jnp.dot(high_ref[...], high, preferred_element_type=F32)
-        out += jnp.dot(high_ref[...], low, preferred_element_type=F32)
-        out += jnp.dot(low_ref[...], high, preferred_element_type=F32)
-        out_ref[:, level] = out.reshape(MEMBERS, TILE_LAT, LANES)
-
-
-def update(weights, forecast):
+PART = 8
+PARTS = LEVELS // PART
+
+
+def update_kernel(
+    weights_ref, prior_ref, innovation_ref, forecast_ref, out_ref, prior_out, innovation_out,
+    high_ref, low_ref, updated_ref, store_sem,
+):
+    def store(i):
+        levels = pl.ds(i * PART, PART)
+        return pltpu.make_async_copy(updated_ref.at[:, levels], out_ref.at[:, levels], store_sem.at[i])
+
+    prior_out[...] = prior_ref[...]
+    innovation_out[...] = innovation_ref[...]
     size = MEMBERS * TILE_LAT
-    block = pl.BlockSpec((MEMBERS, LEVEL_STEP, TILE_LAT, LANES), lambda i: (0, i, 0, 0))
+    tall = jnp.concatenate(
+        [jnp.broadcast_to(weights_ref[b : b + 1, :], (TILE_LAT, LANES)) for b in range(MEMBERS)], axis=0
+    )
+    rows = lax.broadcasted_iota(jnp.int32, (LANES, size), 0)
+    lanes = lax.broadcasted_iota(jnp.int32, (LANES, size), 1)
+    spread = (lanes // TILE_LAT + 64 == rows).astype(BF16)
+    r = lax.broadcasted_iota(jnp.int32, (size, size), 0)
+    c = lax.broadcasted_iota(jnp.int32, (size, size), 1)
+    same = lax.rem(r, TILE_LAT) == lax.rem(c, TILE_LAT)
+    high = tall.astype(BF16)
+    low = (tall - high.astype(F32)).astype(BF16)
+    for part, ref in ((high, high_ref), (low, low_ref)):
+        wide = jnp.dot(part, spread, preferred_element_type=F32)
+        ref[...] = jnp.where(same, wide, 0.0).astype(BF16)
+
+    for step in range(PARTS):
+        for level in range(step * PART, (step + 1) * PART, 2):
+            values = jnp.concatenate(
+                [forecast_ref[:, level + i].reshape(MEMBERS * TILE_LAT, LANES) for i in range(2)], axis=1
+            )
+            high = values.astype(BF16)
+            low = (values - high.astype(F32)).astype(BF16)
+            out = jnp.dot(high_ref[...], high, preferred_element_type=F32)
+            out += jnp.dot(high_ref[...], low, preferred_element_type=F32)
+            out += jnp.dot(low_ref[...], high, preferred_element_type=F32)
+            for i in range(2):
+                updated_ref[:, level + i] = out[:, i * LANES : (i + 1) * LANES].reshape(MEMBERS, TILE_LAT, LANES)
+
+        store(step).start()
+    for i in range(PARTS):
+        store(i).wait()
+
+
+def update(weights, prior, innovation, forecast):
+    size = MEMBERS * TILE_LAT
+    vmem = pl.BlockSpec(memory_space=VMEM)
+    hbm = pl.BlockSpec(memory_space=pltpu.HBM)
+    field = VMEM(forecast.shape, F32)
+    dma = pltpu.SemaphoreType.DMA
     return pl.pallas_call(
         update_kernel,
-        grid=(LEVELS // LEVEL_STEP,),
-        out_shape=jax.ShapeDtypeStruct(forecast.shape, F32),
-        in_specs=[pl.BlockSpec((MEMBERS, LANES), lambda i: (0, 0)), block],
-        out_specs=block,
-        scratch_shapes=[VMEM((size, size), BF16), VMEM((size, size), BF16)],
-        compiler_params=pltpu.CompilerParams(vmem_limit_bytes=16 * 2**20),
+        out_shape=tuple(jax.ShapeDtypeStruct(v.shape, F32) for v in (forecast, prior, innovation)),
+        in_specs=[vmem] * 4,
+        out_specs=(hbm, vmem, vmem),
+        scratch_shapes=[VMEM((size, size), BF16)] * 2 + [field, dma((PARTS,))],
+        compiler_params=pltpu.CompilerParams(vmem_limit_bytes=24 * 2**20),
         name="update",
-    )(weights, forecast)
+    )(weights, prior, innovation, forecast)
 
 
 def per_device(
@@ -505,7 +520,8 @@
     n, content = forecast(sample_deviations, east_courant, north_courant, production, loss_rate)
     summed = ray_sums(entry_count, entry_row, entry_block, content, path_weight)
     prior, innovation, weights = analysis(summed, observed, obs_var)
-    return update(weights, n), prior, innovation.reshape(4 * LANES)
+    updated, prior, innovation = update(weights, prior, innovation, n)
+    return updated, prior, innovation.reshape(4 * LANES)
 
 
 def solution(mesh):

time: 119 us -> 110 us (0.924)
  Pallas kernels: 113 us -> 108 us
  local copies, waits for them, and re-layouts: 4.24 us -> 0.02 us
    unnamed x16 -> x10, local copies, waits for them, and re-layouts: 4.24 us -> 0.02 us
    pallas_call x1, Pallas kernels: 6.59 us -> 3.6 us  [update(): pl.pallas_call(update_kernel, out_shape=tuple((jax.ShapeDtypeStruct(v.sha...]
    pallas_call x1, Pallas kernels: 55.9 us -> 54.4 us  [forecast(): pl.pallas_call(forecast_kernel, out_shape=(jax.ShapeDtypeStruct(n.shape,...]
    pallas_call x1, Pallas kernels: 49.9 us -> 48.6 us  [analysis(): pl.pallas_call(analysis_kernel, out_shape=(jax.ShapeDtypeStruct((MEMBERS,...]
where the time goes in v3:
time: 110 us
  Pallas kernels  108 us (98%)
  between operations  1.49 us (1%)
  other arithmetic  1.14 us (1%)
    pallas_call x1, Pallas kernels, forecast(): pl.pallas_call(forecast_kernel, out_shape=(jax.ShapeDtypeStruct(n.shape,...  54.4 us
    pallas_call x1, Pallas kernels, analysis(): pl.pallas_call(analysis_kernel, out_shape=(jax.ShapeDtypeStruct((MEMBERS,...  48.6 us
    pallas_call x1, Pallas kernels, update(): pl.pallas_call(update_kernel, out_shape=tuple((jax.ShapeDtypeStruct(v.sha...  3.6 us

profile of v3, /device:TPU:1, one launch (start us, length us, event | category | flops | bytes accessed | tf_op | source)
XLA Modules:
  0.0 110.3 jit_solution(3600260832132989356)
XLA Ops:
  0.6 0.0 copy-start
  0.6 0.0 copy-start.4
  0.7 0.0 copy-start.3
  1.4 0.0 copy-start.1
  1.4 0.0 copy-start.2
  1.4 1.1 %pad_maximum_fusion.coefs = f32[4,32,8,128]{3,2,1,0:T(8,128)S(1)} fusion(f32[1,32,8,128]{3,2,1,0:T(8,128)} %bitcast.11, f32[1,32,8,128]{3,2,1,0:T(8,128)} %bitcast.12, f32[1,32,8,128]{3,2,1,0:T(8,128)} %bitcast.13, f32[1,32,8,128]{3,2,1,0:T(8,128)} %bitcast.14), kind=kLoop, calls=%fused_computation | loop fusion | flops 393216 | bytes 1048576 | tf_op jit(solution)/shard_map/stack | solution.py:264
  2.6 54.4 %forecast.1 = (f32[32,32,8,128]{3,2,1,0:T(8,128)S(1)}, bf16[8,32,128]{2,1,0:T(8,128)(2,1)S(1)}) custom-call(f32[4,32,8,128]{3,2,1,0:T(8,128)S(1)} %pad_maximum_fusion.coefs, f32[32,32,8,128]{3,2,1,0:T(8,128)} %n_ref.1), custom_call_target="tpu_custom_call" | custom-call | tf_op jit(solution)/shard_map/forecast/pallas_call | solution.py:247
  57.0 0.0 copy-done
  57.0 0.0 copy-done.4
  57.0 0.0 copy-done.3
  57.0 1.1 ray_sums.1
  58.1 0.0 copy-done.1
  58.1 0.0 copy-done.2
  58.1 48.6 %analysis.1 = (f32[32,512]{1,0:T(8,128)S(1)}, f32[4,128]{1,0:T(4,128)S(1)}, f32[32,128]{1,0:T(8,128)S(1)}) custom-call(f32[4,2,2,128,128]{4,3,2,1,0:T(8,128)S(1)} %bitcast.8, f32[4,128]{1,0:T(4,128)S(1)} %bitcast.9, f32[4,128]{1,0:T(4,128)S(1)} %bitcast.10), custom_call_target="tpu_custom_call" | custom-call | tf_op jit(solution)/shard_map/analysis/pallas_call | solution.py:431
  106.7 3.6 %update.1 = (f32[32,32,8,128]{3,2,1,0:T(8,128)}, f32[32,512]{1,0:T(8,128)}, f32[4,128]{1,0:T(4,128)}) custom-call(f32[32,128]{1,0:T(8,128)S(1)} %get-tuple-element.12.weights_ref, f32[32,512]{1,0:T(8,128)S(1)} %get-tuple-element.13.prior_ref, f32[4,128]{1,0:T(4,128)S(1)} %get-tuple-element.14.innovation_ref, ...), custom_call_target="tpu_custom_call" | custom-call | tf_op jit(solution)/shard_map/update/pallas_call | solution.py:505
Async XLA Ops:
  0.6 56.4 %copy-start = (bf16[48,128,128]{2,1,0:T(8,128)(2,1)S(1)}, bf16[48,128,128]{2,1,0:T(8,128)(2,1)}, u32[]{:S(2)}) copy-start(bf16[48,128,128]{2,1,0:T(8,128)(2,1)} %weight_ref.1) | copy-start | bytes 4718596
  0.6 56.4 %copy-start.4 = (s32[48]{0:T(128)S(1)}, s32[48]{0:T(128)}, u32[]{:S(2)}) copy-start(s32[48]{0:T(128)} %block_ref.1) | copy-start | bytes 580
  0.7 56.4 %copy-start.3 = (s32[48]{0:T(128)S(1)}, s32[48]{0:T(128)}, u32[]{:S(2)}) copy-start(s32[48]{0:T(128)} %row_ref.1) | copy-start | bytes 580
  1.4 56.7 %copy-start.1 = (f32[512]{0:T(512)S(1)}, f32[512]{0:T(512)}, u32[]{:S(2)}) copy-start(f32[512]{0:T(512)} %param.20) | copy-start | bytes 6148
  1.4 56.7 %copy-start.2 = (f32[512]{0:T(512)S(1)}, f32[512]{0:T(512)}, u32[]{:S(2)}) copy-start(f32[512]{0:T(512)} %param.21) | copy-start | bytes 6148

commit v4 on v3

--- a/solution.py
+++ b/solution.py
@@ -289,6 +289,9 @@
     )(entry_count, entry_row, entry_block, content, path_weight)
 
 
+SWEEP = 8
+
+
 def weights_from(total):
     rows = lax.broadcasted_iota(jnp.int32, (MEMBERS, LANES), 0)
     lanes = lax.broadcasted_iota(jnp.int32, (MEMBERS, LANES), 1)
@@ -300,11 +303,16 @@
     pull = jnp.sum(jnp.where(lanes == rows, total[8:9], 0.0), axis=1, keepdims=True)
     work = square + jnp.where(lanes == MEMBERS, pull, 0.0)
     work = work + jnp.where(lanes == rows, MEMBERS - 1.0, 0.0) + jnp.where(lanes == rows + 64, 1.0, 0.0)
-    for j in range(MEMBERS):
-        column = jnp.broadcast_to(work[:, j : j + 1], (MEMBERS, LANES))
-        pivot = column[j : j + 1, :]
-        scale = jnp.where(rows > j, column, 0.0) * (1.0 / pivot)
-        work = work - scale * work[j : j + 1, :]
+    for start in range(0, MEMBERS, SWEEP):
+        columns = [
+            jnp.broadcast_to(work[:, j : j + 1], (MEMBERS, LANES)) for j in range(start, start + SWEEP)
+        ]
+        for k in range(SWEEP):
+            j = start + k
+            scale = jnp.where(rows > j, columns[k], 0.0) * (1.0 / columns[k][j : j + 1, :])
+            for i in range(k + 1, SWEEP):
+                columns[i] = columns[i] - scale * columns[i][j : j + 1, :]
+            work = work - scale * work[j : j + 1, :]
     diagonal = jnp.sum(jnp.where(lanes == rows, work, 0.0), axis=1, keepdims=True)
     work = work / jnp.sqrt(diagonal)
     inverse = jnp.where(inverse_lanes, work, 0.0)
@@ -343,10 +351,16 @@
     barrier = pltpu.get_barrier_semaphore()
     for peer in peers:
         pl.semaphore_signal(barrier, inc=1, device_id=peer, device_id_type=MESH)
-    order = (2, 1, 3, 0)
+    pieces = [(j, t) for t in (0, 1) for j in (2, 1, 3, 0)]
+
+    def part_of(t):
+        return z_hi if t else 1 - z_hi
+
     local = []
-    for j in order:
-        copy = pltpu.make_async_copy(summed_ref.at[lax.rem(x + j, 4), :, core], own.at[j], own_sem.at[j])
+    for j, t in pieces:
+        copy = pltpu.make_async_copy(
+            summed_ref.at[lax.rem(x + j, 4), part_of(t), core], own.at[j, t], own_sem.at[j, t]
+        )
         copy.start()
         local.append(copy)
     pl.semaphore_wait(barrier, len(peers))
@@ -359,22 +373,29 @@
         return copy
 
     core_copies = [
-        send(summed_ref.at[lax.rem(x + j, 4), :, 1 - core], from_core.at[j], core_send.at[j], core_recv.at[j], core_peer)
-        for j in order
+        send(
+            summed_ref.at[lax.rem(x + j, 4), part_of(t), 1 - core], from_core.at[j, t],
+            core_send.at[j, t], core_recv.at[j, t], core_peer,
+        )
+        for j, t in pieces
     ]
     x_copies = []
-    for i, j in enumerate(order):
+    for i, (j, t) in enumerate(pieces):
         local[i].wait()
         core_copies[i].wait_recv()
-        own[j] = own[j] + from_core[j]
+        own[j, t] = own[j, t] + from_core[j, t]
         if j:
-            x_copies.append(send(own.at[j], from_x.at[j - 1], x_send.at[j - 1], x_recv.at[j - 1], x_peer(j)))
-    for copy in x_copies:
+            place = (j - 1, t)
+            x_copies.append(send(own.at[j, t], from_x.at[place], x_send.at[place], x_recv.at[place], x_peer(j)))
+    for copy in x_copies[:3]:
         copy.wait_recv()
-    half[...] = own[0] + from_x[0] + from_x[1] + from_x[2]
-    z_copy = send(half.at[1 - z_hi], from_z, z_send, z_recv, z_peer(4))
+    half[0] = own[0, 0] + from_x[0, 0] + from_x[1, 0] + from_x[2, 0]
+    z_copy = send(half.at[0], from_z, z_send, z_recv, z_peer(4))
+    for copy in x_copies[3:]:
+        copy.wait_recv()
+    half[1] = own[0, 1] + from_x[0, 1] + from_x[1, 1] + from_x[2, 1]
     z_copy.wait_recv()
-    samples = half[z_hi] + from_z[...]
+    samples = half[1] + from_z[...]
 
     spreads, scaled = [], []
     for b in range(4):
@@ -442,7 +463,7 @@
         ]
         + [VMEM((9, LANES), F32)] * 3
         + [VMEM((n, 9, LANES), F32) for n in (7, 3, 7)]
-        + [dma((4,)), dma((4,)), dma((4,)), dma((3,)), dma((3,)), dma, dma, dma((17,)), dma((17,))],
+        + [dma((4, 2)), dma((4, 2)), dma((4, 2)), dma((3, 2)), dma((3, 2)), dma, dma, dma((17,)), dma((17,))],
         compiler_params=pltpu.CompilerParams(collective_id=1, has_side_effects=True, vmem_limit_bytes=16 * 2**20),
         name="analysis",
     )(summed.reshape(4, 2, 2, 4 * MEMBERS, LANES), observed.reshape(4, LANES), obs_var.reshape(4, LANES))

time: 110 us -> 106 us (0.964)
  Pallas kernels: 108 us -> 104 us
    pallas_call x1, Pallas kernels: 48.6 us -> 44.5 us  [analysis(): pl.pallas_call(analysis_kernel, out_shape=(jax.ShapeDtypeStruct((MEMBERS,...]
where the time goes in v4:
time: 106 us
  Pallas kernels  104 us (98%)
  between operations  1.49 us (1%)
  other arithmetic  1.14 us (1%)
    pallas_call x1, Pallas kernels, forecast(): pl.pallas_call(forecast_kernel, out_shape=(jax.ShapeDtypeStruct(n.shape,...  54.4 us
    pallas_call x1, Pallas kernels, analysis(): pl.pallas_call(analysis_kernel, out_shape=(jax.ShapeDtypeStruct((MEMBERS,...  44.5 us
    pallas_call x1, Pallas kernels, update(): pl.pallas_call(update_kernel, out_shape=tuple((jax.ShapeDtypeStruct(v.sha...  3.59 us

profile of v4, /device:TPU:1, one launch (start us, length us, event | category | flops | bytes accessed | tf_op | source)
XLA Modules:
  0.0 106.2 jit_solution(7764907210377567802)
XLA Ops:
  0.6 0.0 copy-start
  0.6 0.0 copy-start.4
  0.7 0.0 copy-start.3
  1.4 0.0 copy-start.1
  1.4 0.0 copy-start.2
  1.4 1.1 %pad_maximum_fusion.coefs = f32[4,32,8,128]{3,2,1,0:T(8,128)S(1)} fusion(f32[1,32,8,128]{3,2,1,0:T(8,128)} %bitcast.11, f32[1,32,8,128]{3,2,1,0:T(8,128)} %bitcast.12, f32[1,32,8,128]{3,2,1,0:T(8,128)} %bitcast.13, f32[1,32,8,128]{3,2,1,0:T(8,128)} %bitcast.14), kind=kLoop, calls=%fused_computation | loop fusion | flops 393216 | bytes 1048576 | tf_op jit(solution)/shard_map/stack | solution.py:264
  2.6 54.4 %forecast.1 = (f32[32,32,8,128]{3,2,1,0:T(8,128)S(1)}, bf16[8,32,128]{2,1,0:T(8,128)(2,1)S(1)}) custom-call(f32[4,32,8,128]{3,2,1,0:T(8,128)S(1)} %pad_maximum_fusion.coefs, f32[32,32,8,128]{3,2,1,0:T(8,128)} %n_ref.1), custom_call_target="tpu_custom_call" | custom-call | tf_op jit(solution)/shard_map/forecast/pallas_call | solution.py:247
  57.0 0.0 copy-done
  57.0 0.0 copy-done.4
  57.0 0.0 copy-done.3
  57.0 1.1 %ray_sums.1 = f32[64,32,128]{2,1,0:T(8,128)S(1)} custom-call(s32[1]{0:T(128)S(6)} %copy.14.count_ref, s32[48]{0:T(128)S(1)} %copy-done.3, s32[48]{0:T(128)S(1)} %copy-done.4, bf16[8,32,128]{2,1,0:T(8,128)(2,1)S(1)} %get-tuple-element.11.content_ref, bf16[48,128,128]{2,1,0:T(8,128)(2,1)S(1)} %copy-done), custom_call_target="tpu_custom_call" | custom-call | tf_op jit(solution)/shard_map/ray_sums/pallas_call | solution.py:281
  58.1 0.0 copy-done.1
  58.1 0.0 copy-done.2
  58.1 44.5 %analysis.1 = (f32[32,512]{1,0:T(8,128)S(1)}, f32[4,128]{1,0:T(4,128)S(1)}, f32[32,128]{1,0:T(8,128)S(1)}) custom-call(f32[4,2,2,128,128]{4,3,2,1,0:T(8,128)S(1)} %bitcast.8, f32[4,128]{1,0:T(4,128)S(1)} %bitcast.9, f32[4,128]{1,0:T(4,128)S(1)} %bitcast.10), custom_call_target="tpu_custom_call" | custom-call | tf_op jit(solution)/shard_map/analysis/pallas_call | solution.py:452
  102.6 3.6 %update.1 = (f32[32,32,8,128]{3,2,1,0:T(8,128)}, f32[32,512]{1,0:T(8,128)}, f32[4,128]{1,0:T(4,128)}) custom-call(f32[32,128]{1,0:T(8,128)S(1)} %get-tuple-element.12.weights_ref, f32[32,512]{1,0:T(8,128)S(1)} %get-tuple-element.13.prior_ref, f32[4,128]{1,0:T(4,128)S(1)} %get-tuple-element.14.innovation_ref, ...), custom_call_target="tpu_custom_call" | custom-call | tf_op jit(solution)/shard_map/update/pallas_call | solution.py:526
Async XLA Ops:
  0.6 56.4 %copy-start = (bf16[48,128,128]{2,1,0:T(8,128)(2,1)S(1)}, bf16[48,128,128]{2,1,0:T(8,128)(2,1)}, u32[]{:S(2)}) copy-start(bf16[48,128,128]{2,1,0:T(8,128)(2,1)} %weight_ref.1) | copy-start | bytes 4718596
  0.6 56.4 %copy-start.4 = (s32[48]{0:T(128)S(1)}, s32[48]{0:T(128)}, u32[]{:S(2)}) copy-start(s32[48]{0:T(128)} %block_ref.1) | copy-start | bytes 580
  0.7 56.4 %copy-start.3 = (s32[48]{0:T(128)S(1)}, s32[48]{0:T(128)}, u32[]{:S(2)}) copy-start(s32[48]{0:T(128)} %row_ref.1) | copy-start | bytes 580
  1.4 56.7 %copy-start.1 = (f32[512]{0:T(512)S(1)}, f32[512]{0:T(512)}, u32[]{:S(2)}) copy-start(f32[512]{0:T(512)} %param.20) | copy-start | bytes 6148
  1.4 56.7 %copy-start.2 = (f32[512]{0:T(512)S(1)}, f32[512]{0:T(512)}, u32[]{:S(2)}) copy-start(f32[512]{0:T(512)} %param.21) | copy-start | bytes 6148

commit v5 on v4

--- a/solution.py
+++ b/solution.py
@@ -23,13 +23,14 @@
 CHUNK = LEVELS // CHUNKS
 BATCH = 32
 PAIRS = MEMBERS // 2
+EARLY = 1
 
 
 def forecast_kernel(
     coefs, n_ref, out_ref, content_ref,
-    own, beyond, edges, to_east, to_west, edges_west, edges_east, beyond_west, beyond_east,
+    own, first, beyond, beyond_first, edge_coef, edges, to_east, to_west, edges_west, edges_east, beyond_west, beyond_east,
     coef_edges, coef_west, coef_east, coef_beyond, frame0, frame_beyond, frame1, total,
-    load_sem, small_send, small_recv, up_send, up_recv, down_send, down_recv,
+    load_sem, small_send, small_recv, up0, up0_recv, up1, up1_recv, down0, down0_recv, down1, down1_recv,
 ):
     lon, lat = lax.axis_index("lon"), lax.axis_index("lat")
     east, west = lax.rem(lon + 1, 16), lax.rem(lon + 15, 16)
@@ -46,23 +47,24 @@
 
     def clear(part):
         size = part.size
-        coef_beyond[:, :, part] = jnp.zeros((4, LEVELS, size, LANES), F32)
+        coef_beyond[:, part] = jnp.zeros((LEVELS, size, LANES), F32)
         beyond_west[:, part] = jnp.zeros((PAIRS, size, LANES), F32)
         beyond_east[:, part] = jnp.zeros((PAIRS, size, LANES), F32)
 
         @pl.loop(0, MEMBERS)
         def _(m):
             beyond[m, :, part] = jnp.zeros((LEVELS, size, LANES), F32)
-
-    clear(pl.ds(2, TILE_LAT - 4))
+            beyond_first[m, :, part] = jnp.zeros((LEVELS, size, LANES), F32)
+
+    clear(pl.ds(1, TILE_LAT - 2))
 
     @pl.when(lat == 15)
     def _():
-        clear(pl.ds(0, 2))
+        clear(pl.ds(0, 1))
 
     @pl.when(lat == 0)
     def _():
-        clear(pl.ds(TILE_LAT - 2, 2))
+        clear(pl.ds(TILE_LAT - 1, 1))
 
     lanes = lax.broadcasted_iota(jnp.int32, (TILE_LAT, LANES), 1)
     rows = lax.broadcasted_iota(jnp.int32, (TILE_LAT, LANES), 0)
@@ -76,12 +78,15 @@
         return out
 
     coef_edges[...] = packed(coefs, pl.ds(0, 4))
+    speed = coefs[1]
+    leaves = (is_first & (speed > 0.0)) | (is_last & (speed < 0.0))
+    edge_coef[...] = jnp.where(leaves, (1.0 - coefs[3]) * jnp.abs(speed), 0.0)
     for i, item in enumerate(loads):
         item.wait()
         edges[half[i]] = packed(own, half[i])
-    first, second = edges[half[0]], edges[half[1]]
-    to_east[...] = jnp.where(slot < 2, first, pltpu.roll(second, 2, 2))
-    to_west[...] = jnp.where(slot >= 2, first, pltpu.roll(second, LANES - 2, 2))
+    front, back = edges[half[0]], edges[half[1]]
+    to_east[...] = jnp.where(slot < 2, front, pltpu.roll(back, 2, 2))
+    to_west[...] = jnp.where(slot >= 2, front, pltpu.roll(back, LANES - 2, 2))
     pl.semaphore_wait(barrier, 8)
 
     def copy(src, dst, send_sem, recv_sem, peer):
@@ -102,23 +107,36 @@
     up = [
         small(4, to_east.at[:, last], beyond_west.at[:, last], (east, north)),
         small(5, to_west.at[:, last], beyond_east.at[:, last], (west, north)),
-        small(6, coefs.at[:, :, last], coef_beyond.at[:, :, last], (lon, north)),
+        small(6, edge_coef.at[:, last], coef_beyond.at[:, last], (lon, north)),
     ]
     down = [
         small(7, to_east.at[:, initial], beyond_west.at[:, initial], (east, south)),
         small(8, to_west.at[:, initial], beyond_east.at[:, initial], (west, south)),
-        small(9, coefs.at[:, :, initial], coef_beyond.at[:, :, initial], (lon, south)),
+        small(9, edge_coef.at[:, initial], coef_beyond.at[:, initial], (lon, south)),
     ]
 
-    def bulk_up(q):
+    def bulk(src, dst, q, row, send_sem, recv_sem, peer):
         levels = pl.ds(q * CHUNK, CHUNK)
-        part = pl.ds(TILE_LAT - 2, 2)
-        return copy(n_ref.at[:, levels, part], beyond.at[:, levels, part], up_send.at[q], up_recv.at[q], (lon, north))
-
-    def bulk_down(q):
-        levels = pl.ds(q * CHUNK, CHUNK)
-        part = pl.ds(0, 2)
-        return copy(n_ref.at[:, levels, part], beyond.at[:, levels, part], down_send.at[q], down_recv.at[q], (lon, south))
+        return copy(src.at[:, levels, row], dst.at[:, levels, row], send_sem.at[q], recv_sem.at[q], (lon, peer))
+
+    fields = ((own, beyond), (first, beyond_first))
+    up_sems = ((up0, up0_recv), (up1, up1_recv))
+    down_sems = ((down0, down0_recv), (down1, down1_recv))
+
+    def bulk_up(q, which):
+        return bulk(*fields[which], q, last, *up_sems[which], north)
+
+    def bulk_down(q, which):
+        return bulk(*fields[which], q, initial, *down_sems[which], south)
+
+    def start_bulk(q, which):
+        @pl.when(has_north)
+        def _():
+            bulk_up(q, which).start()
+
+        @pl.when(has_south)
+        def _():
+            bulk_down(q, which).start()
 
     for item in across:
         item.start()
@@ -133,18 +151,14 @@
         for item in down:
             item.start()
 
-    for q in range(CHUNKS):
-
-        @pl.when(has_north)
-        def _():
-            bulk_up(q).start()
-
-        @pl.when(has_south)
-        def _():
-            bulk_down(q).start()
+    for q in range(EARLY):
+        start_bulk(q, 0)
 
     for item in across:
         item.wait()
+
+    for q in range(EARLY, CHUNKS):
+        start_bulk(q, 0)
 
     @pl.when(has_south)
     def _():
@@ -190,29 +204,50 @@
         frame1[part] = step(frame, west_cell, east_cell, outside, edge_prep)
     total[...] = jnp.zeros_like(total)
 
+    def level_prep(level):
+        return prepared(*[coefs[k, level] for k in range(4)]), lax.rem(2 * LANES - 2 - 4 * level, LANES)
+
+    def exchanged_rows(values):
+        return jnp.where(is_first, pltpu.roll(values, 1, 1), pltpu.roll(values, TILE_LAT - 1, 1))
+
+    @pl.loop(0, CHUNKS)
+    def _(q):
+        @pl.loop(0, CHUNK)
+        def _(i):
+            level = q * CHUNK + i
+            prep, shift = level_prep(level)
+
+            @pl.loop(0, MEMBERS // BATCH)
+            def _(g):
+                part = pl.ds(g * BATCH, BATCH)
+                frame = pltpu.roll(frame0[part], shift, 2)
+                first[part, level] = framed_step(own[part, level], frame, 0.0, prep)
+
+        start_bulk(q, 1)
+
     @pl.loop(0, CHUNKS)
     def _(q):
         @pl.when(has_south)
         def _():
-            bulk_up(q).wait_recv()
+            for which in (0, 1):
+                bulk_up(q, which).wait_recv()
 
         @pl.when(has_north)
         def _():
-            bulk_down(q).wait_recv()
+            for which in (0, 1):
+                bulk_down(q, which).wait_recv()
 
         @pl.loop(0, CHUNK)
         def _(i):
             level = q * CHUNK + i
-            prep = prepared(*[coefs[k, level] for k in range(4)])
-            prep_beyond = prepared(*[coef_beyond[k, level] for k in range(4)])
-            shift = lax.rem(2 * LANES - 2 - 4 * level, LANES)
+            prep, shift = level_prep(level)
+            mine, theirs = edge_coef[level], coef_beyond[level]
 
             @pl.loop(0, MEMBERS // BATCH)
             def _(g):
                 part = pl.ds(g * BATCH, BATCH)
-                n, out = own[part, level], beyond[part, level]
-                n1 = framed_step(n, pltpu.roll(frame0[part], shift, 2), out, prep)
-                out1 = framed_step(out, pltpu.roll(frame_beyond[part], shift, 2), n, prep_beyond)
+                n1 = first[part, level] + mine * exchanged_rows(beyond[part, level])
+                out1 = beyond_first[part, level] + theirs * exchanged_rows(own[part, level])
                 n2 = framed_step(n1, pltpu.roll(frame1[part], shift, 2), out1, prep)
                 out_ref[part, level] = n2
                 total[part] += n2
@@ -226,20 +261,23 @@
         for item in up:
             item.wait_send()
         for q in range(CHUNKS):
-            bulk_up(q).wait_send()
+            for which in (0, 1):
+                bulk_up(q, which).wait_send()
 
     @pl.when(has_south)
     def _():
         for item in down:
             item.wait_send()
         for q in range(CHUNKS):
-            bulk_down(q).wait_send()
+            for which in (0, 1):
+                bulk_down(q, which).wait_send()
 
 
 def forecast(n, east_courant, north_courant, production, loss_rate):
     vmem = pl.BlockSpec(memory_space=VMEM)
     hbm = pl.BlockSpec(memory_space=pltpu.HBM)
     field = VMEM((MEMBERS, LEVELS, TILE_LAT, LANES), F32)
+    levels = VMEM((LEVELS, TILE_LAT, LANES), F32)
     packs = VMEM((MEMBERS, TILE_LAT, LANES), F32)
     pairs = VMEM((PAIRS, TILE_LAT, LANES), F32)
     coef_packs = VMEM((4, TILE_LAT, LANES), F32)
@@ -252,13 +290,14 @@
         ),
         in_specs=[vmem, hbm],
         out_specs=(vmem, vmem),
-        scratch_shapes=[field] * 2
+        scratch_shapes=[field] * 4
+        + [levels]
         + [packs] + [pairs] * 6
         + [coef_packs] * 3
-        + [VMEM((4, LEVELS, TILE_LAT, LANES), F32)]
+        + [levels]
         + [packs] * 4
         + [dma((2,)), dma((10,)), dma((10,))]
-        + [dma((CHUNKS,))] * 4,
+        + [dma((CHUNKS,))] * 8,
         compiler_params=pltpu.CompilerParams(collective_id=2, has_side_effects=True, vmem_limit_bytes=46 * 2**20),
         name="forecast",
     )(jnp.stack([east_courant, north_courant, production, loss_rate]), n)

time: 106 us -> 100 us (0.943)
  Pallas kernels: 104 us -> 97.1 us
    pallas_call x1, Pallas kernels: 44.5 us -> 39.9 us  [analysis(): pl.pallas_call(analysis_kernel, out_shape=(jax.ShapeDtypeStruct((MEMBERS,...]
    pallas_call x1, Pallas kernels: 54.4 us -> 52.5 us  [forecast(): pl.pallas_call(forecast_kernel, out_shape=(jax.ShapeDtypeStruct(n.shape,...]
where the time goes in v5:
time: 100 us; the launch traced here: 99.7 us
  Pallas kernels  97.1 us (97%)
  between operations  1.49 us (1%)
  other arithmetic  1.14 us (1%)
    pallas_call x1, Pallas kernels, forecast(): pl.pallas_call(forecast_kernel, out_shape=(jax.ShapeDtypeStruct(n.shape,...  52.5 us
    pallas_call x1, Pallas kernels, analysis(): pl.pallas_call(analysis_kernel, out_shape=(jax.ShapeDtypeStruct((MEMBERS,...  39.9 us
    pallas_call x1, Pallas kernels, update(): pl.pallas_call(update_kernel, out_shape=tuple((jax.ShapeDtypeStruct(v.sha...  3.59 us

profile of v5, /device:TPU:1, one launch (start us, length us, event | category | flops | bytes accessed | tf_op | source)
XLA Modules:
  0.0 99.7 jit_solution(11194901717441200013)
XLA Ops:
  0.6 0.0 copy-start
  0.6 0.0 copy-start.4
  0.7 0.0 copy-start.3
  1.4 0.0 copy-start.1
  1.4 0.0 copy-start.2
  1.4 1.1 %pad_maximum_fusion.coefs = f32[4,32,8,128]{3,2,1,0:T(8,128)S(1)} fusion(f32[1,32,8,128]{3,2,1,0:T(8,128)} %bitcast.11, f32[1,32,8,128]{3,2,1,0:T(8,128)} %bitcast.12, f32[1,32,8,128]{3,2,1,0:T(8,128)} %bitcast.13, f32[1,32,8,128]{3,2,1,0:T(8,128)} %bitcast.14), kind=kLoop, calls=%fused_computation | loop fusion | flops 393216 | bytes 1048576 | tf_op jit(solution)/shard_map/stack | solution.py:303
  2.6 52.5 %forecast.1 = (f32[32,32,8,128]{3,2,1,0:T(8,128)S(1)}, bf16[8,32,128]{2,1,0:T(8,128)(2,1)S(1)}) custom-call(f32[4,32,8,128]{3,2,1,0:T(8,128)S(1)} %pad_maximum_fusion.coefs, f32[32,32,8,128]{3,2,1,0:T(8,128)} %n_ref.1), custom_call_target="tpu_custom_call" | custom-call | tf_op jit(solution)/shard_map/forecast/pallas_call | solution.py:285
  55.1 0.0 copy-done
  55.1 0.0 copy-done.4
  55.1 0.0 copy-done.3
  55.1 1.1 %ray_sums.1 = f32[64,32,128]{2,1,0:T(8,128)S(1)} custom-call(s32[1]{0:T(128)S(6)} %copy.14.count_ref, s32[48]{0:T(128)S(1)} %copy-done.3, s32[48]{0:T(128)S(1)} %copy-done.4, bf16[8,32,128]{2,1,0:T(8,128)(2,1)S(1)} %get-tuple-element.11.content_ref, bf16[48,128,128]{2,1,0:T(8,128)(2,1)S(1)} %copy-done), custom_call_target="tpu_custom_call" | custom-call | tf_op jit(solution)/shard_map/ray_sums/pallas_call | solution.py:320
  56.2 0.0 copy-done.1
  56.2 0.0 copy-done.2
  56.2 39.9 %analysis.1 = (f32[32,512]{1,0:T(8,128)S(1)}, f32[4,128]{1,0:T(4,128)S(1)}, f32[32,128]{1,0:T(8,128)S(1)}) custom-call(f32[4,2,2,128,128]{4,3,2,1,0:T(8,128)S(1)} %bitcast.8, f32[4,128]{1,0:T(4,128)S(1)} %bitcast.9, f32[4,128]{1,0:T(4,128)S(1)} %bitcast.10), custom_call_target="tpu_custom_call" | custom-call | tf_op jit(solution)/shard_map/analysis/pallas_call | solution.py:491
  96.1 3.6 %update.1 = (f32[32,32,8,128]{3,2,1,0:T(8,128)}, f32[32,512]{1,0:T(8,128)}, f32[4,128]{1,0:T(4,128)}) custom-call(f32[32,128]{1,0:T(8,128)S(1)} %get-tuple-element.12.weights_ref, f32[32,512]{1,0:T(8,128)S(1)} %get-tuple-element.13.prior_ref, f32[4,128]{1,0:T(4,128)S(1)} %get-tuple-element.14.innovation_ref, ...), custom_call_target="tpu_custom_call" | custom-call | tf_op jit(solution)/shard_map/update/pallas_call | solution.py:565
Async XLA Ops:
  0.6 54.4 %copy-start = (bf16[48,128,128]{2,1,0:T(8,128)(2,1)S(1)}, bf16[48,128,128]{2,1,0:T(8,128)(2,1)}, u32[]{:S(2)}) copy-start(bf16[48,128,128]{2,1,0:T(8,128)(2,1)} %weight_ref.1) | copy-start | bytes 4718596
  0.6 54.4 %copy-start.4 = (s32[48]{0:T(128)S(1)}, s32[48]{0:T(128)}, u32[]{:S(2)}) copy-start(s32[48]{0:T(128)} %block_ref.1) | copy-start | bytes 580
  0.7 54.4 %copy-start.3 = (s32[48]{0:T(128)S(1)}, s32[48]{0:T(128)}, u32[]{:S(2)}) copy-start(s32[48]{0:T(128)} %row_ref.1) | copy-start | bytes 580
  1.4 54.8 %copy-start.1 = (f32[512]{0:T(512)S(1)}, f32[512]{0:T(512)}, u32[]{:S(2)}) copy-start(f32[512]{0:T(512)} %param.20) | copy-start | bytes 6148
  1.4 54.8 %copy-start.2 = (f32[512]{0:T(512)S(1)}, f32[512]{0:T(512)}, u32[]{:S(2)}) copy-start(f32[512]{0:T(512)} %param.21) | copy-start | bytes 6148

commit v6 on v5

--- a/solution.py
+++ b/solution.py
@@ -456,7 +456,7 @@
     g0[0:8] = sum(
         pltpu.roll(square[8 * k : 8 * k + 8], MEMBERS * k, 1) if k else square[0:8] for k in range(4)
     )
-    g0[8:9] = gram[MEMBERS : MEMBERS + 1]
+    g0[8:16] = gram[MEMBERS : MEMBERS + 8]
 
     waits = []
     base = 0
@@ -500,8 +500,8 @@
         scratch_shapes=[
             VMEM((4,) + piece, F32), VMEM((4,) + piece, F32), VMEM((3,) + piece, F32), VMEM(piece, F32), VMEM(piece[1:], F32),
         ]
-        + [VMEM((9, LANES), F32)] * 3
-        + [VMEM((n, 9, LANES), F32) for n in (7, 3, 7)]
+        + [VMEM((16, LANES), F32)] * 3
+        + [VMEM((n, 16, LANES), F32) for n in (7, 3, 7)]
         + [dma((4, 2)), dma((4, 2)), dma((4, 2)), dma((3, 2)), dma((3, 2)), dma, dma, dma((17,)), dma((17,))],
         compiler_params=pltpu.CompilerParams(collective_id=1, has_side_effects=True, vmem_limit_bytes=16 * 2**20),
         name="analysis",

time: 100 us -> 100 us (level)
  no operation moved by 1% of the time
where the time goes in v6:
time: 100 us
  Pallas kernels  97.5 us (98%)
  between operations  1.49 us (1%)
  other arithmetic  1.14 us (1%)
    pallas_call x1, Pallas kernels, forecast(): pl.pallas_call(forecast_kernel, out_shape=(jax.ShapeDtypeStruct(n.shape,...  52.5 us
    pallas_call x1, Pallas kernels, analysis(): pl.pallas_call(analysis_kernel, out_shape=(jax.ShapeDtypeStruct((MEMBERS,...  40.4 us
    pallas_call x1, Pallas kernels, update(): pl.pallas_call(update_kernel, out_shape=tuple((jax.ShapeDtypeStruct(v.sha...  3.6 us

profile of v6, /device:TPU:1, one launch (start us, length us, event | category | flops | bytes accessed | tf_op | source)
XLA Modules:
  0.0 100.2 jit_solution(7272610993659258460)
XLA Ops:
  0.6 0.0 copy-start
  0.6 0.0 copy-start.4
  0.7 0.0 copy-start.3
  1.4 0.0 copy-start.1
  1.4 0.0 copy-start.2
  1.4 1.1 %pad_maximum_fusion.coefs = f32[4,32,8,128]{3,2,1,0:T(8,128)S(1)} fusion(f32[1,32,8,128]{3,2,1,0:T(8,128)} %bitcast.11, f32[1,32,8,128]{3,2,1,0:T(8,128)} %bitcast.12, f32[1,32,8,128]{3,2,1,0:T(8,128)} %bitcast.13, f32[1,32,8,128]{3,2,1,0:T(8,128)} %bitcast.14), kind=kLoop, calls=%fused_computation | loop fusion | flops 393216 | bytes 1048576 | tf_op jit(solution)/shard_map/stack | solution.py:303
  2.6 52.5 %forecast.1 = (f32[32,32,8,128]{3,2,1,0:T(8,128)S(1)}, bf16[8,32,128]{2,1,0:T(8,128)(2,1)S(1)}) custom-call(f32[4,32,8,128]{3,2,1,0:T(8,128)S(1)} %pad_maximum_fusion.coefs, f32[32,32,8,128]{3,2,1,0:T(8,128)} %n_ref.1), custom_call_target="tpu_custom_call" | custom-call | tf_op jit(solution)/shard_map/forecast/pallas_call | solution.py:285
  55.1 0.0 copy-done
  55.1 0.0 copy-done.4
  55.1 0.0 copy-done.3
  55.1 1.1 %ray_sums.1 = f32[64,32,128]{2,1,0:T(8,128)S(1)} custom-call(s32[1]{0:T(128)S(6)} %copy.14.count_ref, s32[48]{0:T(128)S(1)} %copy-done.3, s32[48]{0:T(128)S(1)} %copy-done.4, bf16[8,32,128]{2,1,0:T(8,128)(2,1)S(1)} %get-tuple-element.11.content_ref, bf16[48,128,128]{2,1,0:T(8,128)(2,1)S(1)} %copy-done), custom_call_target="tpu_custom_call" | custom-call | tf_op jit(solution)/shard_map/ray_sums/pallas_call | solution.py:320
  56.2 0.0 copy-done.1
  56.2 0.0 copy-done.2
  56.2 40.4 %analysis.1 = (f32[32,512]{1,0:T(8,128)S(1)}, f32[4,128]{1,0:T(4,128)S(1)}, f32[32,128]{1,0:T(8,128)S(1)}) custom-call(f32[4,2,2,128,128]{4,3,2,1,0:T(8,128)S(1)} %bitcast.8, f32[4,128]{1,0:T(4,128)S(1)} %bitcast.9, f32[4,128]{1,0:T(4,128)S(1)} %bitcast.10), custom_call_target="tpu_custom_call" | custom-call | tf_op jit(solution)/shard_map/analysis/pallas_call | solution.py:491
  96.6 3.6 %update.1 = (f32[32,32,8,128]{3,2,1,0:T(8,128)}, f32[32,512]{1,0:T(8,128)}, f32[4,128]{1,0:T(4,128)}) custom-call(f32[32,128]{1,0:T(8,128)S(1)} %get-tuple-element.12.weights_ref, f32[32,512]{1,0:T(8,128)S(1)} %get-tuple-element.13.prior_ref, f32[4,128]{1,0:T(4,128)S(1)} %get-tuple-element.14.innovation_ref, ...), custom_call_target="tpu_custom_call" | custom-call | tf_op jit(solution)/shard_map/update/pallas_call | solution.py:565
Async XLA Ops:
  0.6 54.4 %copy-start = (bf16[48,128,128]{2,1,0:T(8,128)(2,1)S(1)}, bf16[48,128,128]{2,1,0:T(8,128)(2,1)}, u32[]{:S(2)}) copy-start(bf16[48,128,128]{2,1,0:T(8,128)(2,1)} %weight_ref.1) | copy-start | bytes 4718596
  0.6 54.4 %copy-start.4 = (s32[48]{0:T(128)S(1)}, s32[48]{0:T(128)}, u32[]{:S(2)}) copy-start(s32[48]{0:T(128)} %block_ref.1) | copy-start | bytes 580
  0.7 54.4 %copy-start.3 = (s32[48]{0:T(128)S(1)}, s32[48]{0:T(128)}, u32[]{:S(2)}) copy-start(s32[48]{0:T(128)} %row_ref.1) | copy-start | bytes 580
  1.4 54.8 %copy-start.1 = (f32[512]{0:T(512)S(1)}, f32[512]{0:T(512)}, u32[]{:S(2)}) copy-start(f32[512]{0:T(512)} %param.20) | copy-start | bytes 6148
  1.4 54.8 %copy-start.2 = (f32[512]{0:T(512)S(1)}, f32[512]{0:T(512)}, u32[]{:S(2)}) copy-start(f32[512]{0:T(512)} %param.21) | copy-start | bytes 6148
